TPU v7x, 32 devices: a whole 2x2x4 slice. The times are simulated.
32 devices in a mesh: member: 2 (over x), lon: 16 (over z, y, core).
Axes of the slice: x: 2, y: 2, z: 4, core: 2. Of those that a mesh axis runs over, the one named last changes fastest.
Arguments:
- surface_old: float32 [1024, 256], P(('member', 'lon')), parts along dimension 0, may hold values from -6 to 6
- surface_forcing: float32 [1024, 256], P(('member', 'lon')), parts along dimension 0, may hold values from -13 to 13
- surface_coeff: float32 [512, 256], P('lon'), may hold values from 0.1 to 1
- ocean_mask: int32 [512, 256], P('lon'), may hold values from 0 to 1, as said below
- column_depth: int32 [256, 512], P('lon'), may hold values from 0 to 16, as said below
- east_depth: int32 [256, 512], P('lon'), may hold values from 0 to 16, as said below
- tracers: float32 [16, 16, 256, 512], P('member', None, 'lon'), parts along dimension 0, may hold values from 0.05 to 2
- u_clinic: float32 [32, 256, 512], P('member', 'lon'), parts along dimension 0, may hold values from -0.9 to 0.9
- v_clinic: float32 [32, 256, 512], P('member', 'lon'), parts along dimension 0, may hold values from -0.9 to 0.9
Outputs:
- surface: float32 [1024, 256], P(('member', 'lon')), parts along dimension 0
- tracers_new: float32 [16, 16, 256, 512], P('member', None, 'lon'), parts along dimension 0
There are 2 independent parts, one for each index of `member`. A program takes and returns all parts, laid end to end along the dimension named above; an argument that names none is the same for every part. Nothing has to cross between parts.
Inputs may be any that keep to these rules, and one draw needn't show every extreme that they name: ocean_mask[j, i] is 1 exactly where column_depth[i, j] is positive, else 0. `column_depth`: 0 marks land. east_depth[i, j] is the smaller of column_depth[i, j] and column_depth[i + 1, j], longitudes periodic.
All inputs are finite; a program needn't handle non-finite values.
Results may differ from a plain program's by a relative error of at most 0.0003.
Values sent between devices are 32-bit elements; how exact they have to be, the bound alone decides.
A program may use at most 64 MiB of HBM per device.

v0:
```python
import jax
import jax.numpy as jnp
from jax import lax
from jax.sharding import PartitionSpec as P

SOLVER_ITERS = 4


BARO_GAIN = 0.1
HORIZ_DIFF = 0.1
VERT_DIFF = 0.15
RATE_CARBON = 0.3
RATE_AMMONIUM = 0.2
RATE_NITRITE = 0.2
RATE_SULFIDE = 0.3
RATE_NITROUS = 0.2
HALF_OXYGEN = 0.3
HALF_NITRATE = 0.3
HALF_NITRITE = 0.3
YIELD_NITROUS = 0.3


def padded_2(block, sides, width, periodic):
    for axis, dim in sides:
        count = lax.axis_size(axis)
        forward = [(i, i + 1) for i in range(count - 1)]
        if periodic:
            forward.append((count - 1, 0))
        backward = [(target, source) for source, target in forward]
        low = lax.ppermute(
            lax.slice_in_dim(block, block.shape[dim] - width, None, axis=dim), axis, forward
        )
        high = lax.ppermute(lax.slice_in_dim(block, 0, width, axis=dim), axis, backward)
        block = jnp.concatenate([low, block, high], axis=dim)
    return block


def apply_operator(values_in, mask_float, coeff):
    masked = mask_float * values_in
    padded = padded_2(masked, (("lon", 0),), 1, False)
    top_device = lax.axis_index("lon") == lax.axis_size("lon") - 1
    folded = jnp.where(top_device, masked[-1:, ::-1], padded[-1:])
    northern = jnp.concatenate([padded[2:-1], folded], axis=0)
    southern = padded[:-2]
    eastern = jnp.roll(masked, -1, axis=1)
    western = jnp.roll(masked, 1, axis=1)
    return (coeff + 4.0 * mask_float) * values_in - mask_float * (
        northern + southern + eastern + western
    )


def squared_total(residual):
    return lax.psum(jnp.sum(residual * residual), "lon")


def plain_solve(right_side, mask_float, coeff):
    solution = jnp.zeros_like(right_side)
    residual = right_side
    direction = right_side
    norm_now = squared_total(residual)
    for sweep in range(SOLVER_ITERS):
        applied = apply_operator(direction, mask_float, coeff)
        curvature = lax.psum(jnp.sum(direction * applied), "lon")
        step_size = norm_now / curvature
        solution = solution + step_size * direction
        residual = residual - step_size * applied
        norm_next = squared_total(residual)
        direction = residual + norm_next / norm_now * direction
        norm_now = norm_next
    return solution


def open_faces(column_depth, east_depth, east_baro, north_baro, u_clinic, v_clinic):
    level_index = lax.broadcasted_iota(jnp.int32, u_clinic.shape, 0)
    wet = (level_index < column_depth[None]).astype(jnp.float32)
    east_open = (level_index < east_depth[None]).astype(jnp.float32)
    north_open = wet * jnp.concatenate([wet[:, :, 1:], jnp.zeros_like(wet[:, :, :1])], axis=2)
    below_open = wet * jnp.concatenate([wet[1:], jnp.zeros_like(wet[:1])], axis=0)
    east_flow = (u_clinic + east_baro[None]) * east_open
    north_flow = (v_clinic + north_baro[None]) * north_open
    return (wet, east_open, north_open, below_open, east_flow, north_flow)


def meridional_vertical(masked, north_flow, north_open, below_open):
    count_rows = masked.shape[-1]
    pad_widths = [(0, 0)] * (masked.ndim - 1) + [(2, 2)]
    padded = jnp.pad(masked, pad_widths)
    south_one = padded[..., 1 : count_rows + 1]
    north_one = padded[..., 3 : count_rows + 3]
    north_two = padded[..., 4 : count_rows + 4]
    face_north = (7.0 * (masked + north_one) - (south_one + north_two)) / 12.0
    flux_north = north_flow * face_north - HORIZ_DIFF * (north_one - masked) * north_open
    flux_south = jnp.concatenate(
        [jnp.zeros_like(flux_north[..., :1]), flux_north[..., :-1]], axis=-1
    )
    below = jnp.concatenate([masked[..., 1:, :, :], jnp.zeros_like(masked[..., :1, :, :])], axis=-3)
    flux_down = VERT_DIFF * (below - masked) * below_open
    flux_up = jnp.concatenate(
        [jnp.zeros_like(flux_down[..., :1, :, :]), flux_down[..., :-1, :, :]], axis=-3
    )
    return flux_south - flux_north + (flux_down - flux_up)


def redox_sources(masked):
    oxygen = masked[0]
    nitrate = masked[1]
    nitrite = masked[2]
    ammonium = masked[3]
    carbon = masked[5]
    sulfide = masked[6]
    nitrous = masked[7]
    breakdown = RATE_CARBON * carbon
    with_oxygen = oxygen / (oxygen + HALF_OXYGEN)
    with_nitrate = (1.0 - with_oxygen) * nitrate / (nitrate + HALF_NITRATE)
    with_nitrite = (1.0 - with_oxygen - with_nitrate) * nitrite / (nitrite + HALF_NITRITE)
    with_sulfate = 1.0 - with_oxygen - with_nitrate - with_nitrite
    first_nitr = RATE_AMMONIUM * ammonium * with_oxygen
    second_nitr = RATE_NITRITE * nitrite * with_oxygen
    sulfide_ox = RATE_SULFIDE * sulfide * with_oxygen
    return jnp.stack(
        [
            -1.3 * breakdown * with_oxygen
            - 1.5 * first_nitr
            - 0.5 * second_nitr
            - 2.0 * sulfide_ox,
            -0.9 * breakdown * with_nitrate + second_nitr,
            0.9 * breakdown * with_nitrate
            - 0.6 * breakdown * with_nitrite
            + (1.0 - YIELD_NITROUS) * first_nitr
            - second_nitr,
            0.15 * breakdown - first_nitr,
            0.1 * breakdown,
            -breakdown,
            0.5 * breakdown * with_sulfate - sulfide_ox,
            YIELD_NITROUS * first_nitr - RATE_NITROUS * nitrous * (1.0 - with_oxygen),
        ]
    )


def body(
    surface_old,
    surface_forcing,
    surface_coeff,
    ocean_mask,
    column_depth,
    east_depth,
    tracers,
    u_clinic,
    v_clinic,
):
    mask_float = ocean_mask.astype(jnp.float32)
    right_side = surface_coeff * surface_old + surface_forcing
    surface = plain_solve(right_side, mask_float, surface_coeff)
    band_flow = -BARO_GAIN * (jnp.roll(surface, -1, axis=1) - surface)
    moved = lax.all_to_all(
        jnp.stack([surface, band_flow]), "lon", split_axis=2, concat_axis=1, tiled=True
    )
    strip_surface = moved[0].T
    east_baro = moved[1].T
    above_surface = jnp.concatenate([strip_surface[:, 1:], strip_surface[:, -1:]], axis=1)
    north_baro = -BARO_GAIN * (above_surface - strip_surface)
    wet, east_open, north_open, below_open, east_flow, north_flow = open_faces(
        column_depth, east_depth, east_baro, north_baro, u_clinic, v_clinic
    )
    masked = tracers * wet[None]
    tracer_count = masked.shape[0]
    columns_here = masked.shape[2]
    stacked = jnp.concatenate([masked, east_flow[None], east_open[None]], axis=0)
    padded = padded_2(stacked, (("lon", 2),), 2, True)
    tracer_pad = padded[:tracer_count]
    west_flow = padded[tracer_count, :, 1:2]
    west_open = padded[tracer_count + 1, :, 1:2]
    flow_all = jnp.concatenate([west_flow, east_flow], axis=1)
    open_all = jnp.concatenate([west_open, east_open], axis=1)
    center = tracer_pad[:, :, 1 : columns_here + 2]
    east_one = tracer_pad[:, :, 2 : columns_here + 3]
    west_one = tracer_pad[:, :, 0 : columns_here + 1]
    east_two = tracer_pad[:, :, 3 : columns_here + 4]
    face_east = (7.0 * (center + east_one) - (west_one + east_two)) / 12.0
    flux_all = flow_all[None] * face_east - HORIZ_DIFF * (east_one - center) * open_all[None]
    conv_east = flux_all[:, :, :-1] - flux_all[:, :, 1:]
    transport = conv_east + meridional_vertical(
        masked, north_flow[None], north_open[None], below_open[None]
    )
    tendency = transport + redox_sources(masked)
    tracers_new = tracers + wet[None] * tendency
    return (surface, tracers_new)


def solution(mesh):
    in_specs = (
        P(("member", "lon"), None),
        P(("member", "lon"), None),
        P("lon", None),
        P("lon", None),
        P("lon", None),
        P("lon", None),
        P("member", None, "lon", None),
        P("member", "lon", None),
        P("member", "lon", None),
    )
    out_specs = (P(("member", "lon"), None), P("member", None, "lon", None))
    return jax.shard_map(body, mesh=mesh, in_specs=in_specs, out_specs=out_specs, check_vma=False)
```

profile of v0, /device:TPU:0, one launch (start us, length us, event | category | flops | bytes accessed | tf_op | source)
XLA Modules:
  0.0 328.7 jit_solution(14252063561252996319)
XLA Ops:
  0.6 0.8 convert_multiply_fusion.3
  1.5 2.4 collective-permute-start.1
  3.8 1.3 collective-permute-start
  5.2 0.8 fusion.20
  6.0 4.9 %copy_multiply_fusion = f32[8,16,16,512]{3,1,2,0:T(8,128)S(1)} fusion(f32[8,16,16,512]{3,2,1,0:T(8,128)} %param.15, f32[16,16,512]{2,0,1:T(8,128)S(1)} %fusion.20), kind=kLoop, calls=%fused_computation.19 | loop fusion | flops 1048576 | bytes 8912896 | tf_op jit(solution)/shard_map/mul | solution.py:165
  11.0 0.4 subtract_dynamic-update-slice_fusion.3
  11.6 0.4 subtract_dynamic-update-slice_fusion.2
  13.2 2.0 copy-done.4
  15.5 0.7 multiply_reduce_fusion.5
  16.3 36.4 %all-reduce.6 = (f32[]{:T(128)}, f32[]{:T(128)}) all-reduce(f32[]{:T(128)} %get-tuple-element.9, f32[]{:T(128)} %get-tuple-element.8), channel_id=1, replica_groups=mesh['member'=2,'lon'=16] {'lon'}, use_global_device_ids=true, to_apply=%region_1.0 | all-reduce | flops 2 | bytes 16 | tf_op jit(solution)/shard_map/psum | solution.py:53
  54.0 0.6 multiply_reduce_fusion.4
  54.8 30.1 %psum.58 = f32[]{:T(128)} all-reduce(f32[]{:T(128)} %multiply_reduce_fusion.4), channel_id=1, replica_groups=mesh['member'=2,'lon'=16] {'lon'}, use_global_device_ids=true, to_apply=%region_5.6 | all-reduce | flops 1 | bytes 8 | tf_op jit(solution)/shard_map/psum | solution.py:53
  86.3 1.3 collective-permute-start.2
  87.7 3.0 collective-permute-start.3
  90.9 0.6 collective-permute-done.3
  91.5 0.7 multiply_reduce_fusion.3
  92.2 31.1 %psum.59 = f32[]{:T(128)} all-reduce(f32[]{:T(128)} %get-tuple-element.20), channel_id=1, replica_groups=mesh['member'=2,'lon'=16] {'lon'}, use_global_device_ids=true, to_apply=%region_7.8 | all-reduce | flops 1 | bytes 8 | tf_op jit(solution)/shard_map/psum | solution.py:63
  124.7 0.6 multiply_reduce_fusion.2
  125.3 30.1 %psum.60 = f32[]{:T(128)} all-reduce(f32[]{:T(128)} %get-tuple-element.18), channel_id=1, replica_groups=mesh['member'=2,'lon'=16] {'lon'}, use_global_device_ids=true, to_apply=%region_9.10 | all-reduce | flops 1 | bytes 8 | tf_op jit(solution)/shard_map/psum | solution.py:53
  156.8 1.3 collective-permute-start.4
  158.2 3.0 collective-permute-start.5
  161.4 0.6 collective-permute-done.5
  162.0 0.7 multiply_reduce_fusion.1
  162.7 31.1 %psum.61 = f32[]{:T(128)} all-reduce(f32[]{:T(128)} %get-tuple-element.14), channel_id=1, replica_groups=mesh['member'=2,'lon'=16] {'lon'}, use_global_device_ids=true, to_apply=%region_11.12 | all-reduce | flops 1 | bytes 8 | tf_op jit(solution)/shard_map/psum | solution.py:63
  195.1 0.6 multiply_reduce_fusion
  195.8 30.1 %psum.62 = f32[]{:T(128)} all-reduce(f32[]{:T(128)} %multiply_reduce_fusion), channel_id=1, replica_groups=mesh['member'=2,'lon'=16] {'lon'}, use_global_device_ids=true, to_apply=%region_13.14 | all-reduce | flops 1 | bytes 8 | tf_op jit(solution)/shard_map/psum | solution.py:53
  227.3 1.3 collective-permute-start.6
  228.7 3.0 collective-permute-start.7
  232.0 0.6 collective-permute-done.7
  232.5 0.7 fusion.29
  233.3 5.0 %slice.315 = f32[8,15,16,512]{3,1,2,0:T(8,128)} slice(f32[8,16,16,512]{3,1,2,0:T(8,128)} %copy-done), slice={[0:8], [1:16], [0:16], [0:512]} | slice | bytes 7864320 | tf_op jit(solution)/shard_map/slice | solution.py:96
  238.3 31.2 %psum.63 = f32[]{:T(128)} all-reduce(f32[]{:T(128)} %fusion.29), channel_id=1, replica_groups=mesh['member'=2,'lon'=16] {'lon'}, use_global_device_ids=true, to_apply=%region_15.16 | all-reduce | flops 1 | bytes 8 | tf_op jit(solution)/shard_map/psum | solution.py:63
  271.2 0.9 reshape.32
  272.1 3.5 %all-to-all-start = ((f32[16,1,1024]{2,1,0:T(1,128)}), f32[16,1,1024]{2,1,0:T(1,128)S(1)}, u32[]{:S(2)}, u32[]{:S(2)}) async-start(f32[16,1,1024]{2,1,0:T(1,128)} %reshape.32), calls=%async_computation | async-start | bytes 131072 | tf_op jit(solution)/shard_map/all_to_all | solution.py:155
  275.6 0.9 fusion.19
  276.5 6.0 %all-to-all-done = f32[16,1,1024]{2,1,0:T(1,128)S(1)} async-done(((f32[16,1,1024]{2,1,0:T(1,128)}), f32[16,1,1024]{2,1,0:T(1,128)S(1)}, u32[]{:S(2)}, u32[]{:S(2)}) %all-to-all-start) | async-done | bytes 65568 | tf_op jit(solution)/shard_map/all_to_all | solution.py:155
  282.5 0.6 broadcast.191
  283.1 0.8 reduce
  285.1 2.6 pad_maximum_fusion.3
  287.7 4.4 %collective-permute-start.9 = (f32[10,16,2,512]{3,1,2,0:T(8,128)}, f32[10,16,2,512]{3,1,2,0:T(8,128)}, u32[]{:S(2)}, u32[]{:S(2)}) collective-permute-start(f32[10,16,2,512]{3,1,2,0:T(8,128)} %get-tuple-element.30), channel_id=1, source_target_pairs={{1,0},{2,1},{3,2},{4,3},{5,4},{6,5},{7,6},{8,7},{9,8},{10,9},{11,1... | collective-permute-start | bytes 1966088 | tf_op jit(solution)/shard_map/ppermute | solution.py:33
  292.2 1.6 fusion.17
  293.8 3.8 %fusion.6 = (f32[8,16,16,512]{3,1,2,0:T(8,128)S(1)}, f32[8,16,16,512]{3,1,2,0:T(8,128)S(1)}) fusion(f32[8,16,16,512]{3,1,2,0:T(8,128)S(1)} %copy-done.1, f32[16,16,512]{2,0,1:T(8,128)S(1)} %get-tuple-element.36, f32[16,16,512]{2,0,1:T(8,128)S(1)} %get-tuple-element.35, f32[16,16,512]{2,0,1:T(8,128)S(1)} %get-tuple-element.39, f32[8,15,16,512]{3,1,2,0:T(8,128)S(1)} %copy-done.2), kind=kLoop, calls=%fused_computation.12 | loop fusion | flops 10485760 | bytes 18087936 | tf_op jit(solution)/shard_map/sub | solution.py:92
  298.0 2.8 collective-permute-done.8
  300.8 0.8 slice_bitcast_fusion.1
  301.8 4.4 %maximum_maximum_fusion = (f32[10,16,18,512]{3,1,2,0:T(8,128)S(1)}, f32[10,16,18,512]{3,1,2,0:T(8,128)}) fusion(f32[1,16,16,512]{3,1,2,0:T(8,128)S(1)} %copy-done.6, f32[1,16,16,512]{3,1,2,0:T(8,128)S(1)} %fusion.64, f32[8,16,16,512]{3,1,2,0:T(8,128)S(1)} %copy-done.1, f32[10,16,2,512]{3,1,2,0:T(8,128)} %collective-permute-done.8, ...), kind=kLoop, calls=%fused_computation | loop fusion | flops 8847360 | bytes 18350080 | tf_op jit(solution)/shard_map/concatenate | solution.py:34
  306.2 6.3 %fusion.2 = f32[8,16,17,512]{3,1,2,0:T(8,128)} fusion(f32[10,16,18,512]{3,1,2,0:T(8,128)} %get-tuple-element.28, f32[10,16,18,512]{3,1,2,0:T(8,128)S(1)} %get-tuple-element.27, f32[16,17,512]{2,0,1:T(8,128)S(1)} %get-tuple-element.65, f32[16,17,512]{2,0,1:T(8,128)S(1)} %get-tuple-element.64), kind=kLoop, calls=%fused_computation.8 | loop fusion | flops 8912896 | bytes 23396352 | tf_op jit(solution)/shard_map/sub | solution.py:180
  312.5 11.7 %fusion.10 = f32[8,16,16,512]{3,1,2,0:T(8,128)S(1)} fusion(f32[8,16,16,512]{3,1,2,0:T(8,128)} %copy-done.4, f32[8,16,17,512]{3,1,2,0:T(8,128)} %fusion.2, f32[8,16,16,512]{3,1,2,0:T(8,128)S(1)} %get-tuple-element.32, f32[8,15,16,512]{3,1,2,0:T(8,128)S(1)} %bitcast.28, f32[8,16,16,512]{3,1,2,0:T(8,128)S(1)} %get-tuple-element.31, ...), kind=kLoop, calls=%fused_computation.17 | loop fusion | flops 8388608 | bytes 38002688 | tf_op jit(solution)/shard_map/add | solution.py:186
  324.2 4.5 %copy.35 = f32[8,16,16,512]{3,2,1,0:T(8,128)} copy(f32[8,16,16,512]{3,1,2,0:T(8,128)S(1)} %fusion.10) | data formatting | bytes 8388608
  (91 shorter events, 5.1 us)
Async XLA Ops:
  1.5 14.0 %collective-permute-start.1 = (f32[1,256]{1,0:T(1,128)S(1)}, f32[1,256]{1,0:T(1,128)S(1)}, u32[]{:S(2)}, u32[]{:S(2)}) collective-permute-start(f32[1,256]{1,0:T(1,128)S(1)} %get-tuple-element.59), channel_id=1, source_target_pairs={{0,1},{1,2},{2,3},{3,4},{4,5},{5,6},{6,7},{7,8},{8,9},{9,10},{10,1... | collective-permute-start | bytes 3080 | tf_op jit(solution)/shard_map/ppermute | solution.py:30
  3.8 11.7 %collective-permute-start = (f32[1,256]{1,0:T(1,128)S(1)}, f32[1,256]{1,0:T(1,128)S(1)}, u32[]{:S(2)}, u32[]{:S(2)}) collective-permute-start(f32[1,256]{1,0:T(1,128)S(1)} %get-tuple-element.58), channel_id=1, source_target_pairs={{1,0},{2,1},{3,2},{4,3},{5,4},{6,5},{7,6},{8,7},{9,8},{10,9},{11,1... | collective-permute-start | bytes 3080 | tf_op jit(solution)/shard_map/ppermute | solution.py:33
  6.0 189.7 %copy-start.3 = (f32[16,16,512]{2,0,1:T(8,128)}, f32[16,16,512]{2,0,1:T(8,128)S(1)}, u32[]{:S(2)}) copy-start(f32[16,16,512]{2,0,1:T(8,128)S(1)} %fusion.20) | copy-start | bytes 1572868
  11.0 1.9 copy-start
  12.3 2.9 copy-start.13
  12.3 3.2 copy-start.10
  12.3 3.2 copy-start.11
  13.1 2.0 copy-start.4
  15.2 269.8 %copy-start.5 = (f32[1,16,16,512]{3,1,2,0:T(8,128)}, f32[1,16,16,512]{3,1,2,0:T(8,128)S(1)}, u32[]{:S(2)}) copy-start(f32[1,16,16,512]{3,1,2,0:T(8,128)S(1)} %fusion.21) | copy-start | bytes 1572868
  86.3 4.6 %collective-permute-start.2 = (f32[1,256]{1,0:T(1,128)S(1)}, f32[1,256]{1,0:T(1,128)S(1)}, u32[]{:S(2)}, u32[]{:S(2)}) collective-permute-start(f32[1,256]{1,0:T(1,128)S(1)} %get-tuple-element.52), channel_id=1, source_target_pairs={{1,0},{2,1},{3,2},{4,3},{5,4},{6,5},{7,6},{8,7},{9,8},{10,9},{11,1... | collective-permute-start | bytes 3080 | tf_op jit(solution)/shard_map/ppermute | solution.py:33
  87.7 3.8 %collective-permute-start.3 = (f32[1,256]{1,0:T(1,128)S(1)}, f32[1,256]{1,0:T(1,128)S(1)}, u32[]{:S(2)}, u32[]{:S(2)}) collective-permute-start(f32[1,256]{1,0:T(1,128)S(1)} %get-tuple-element.53), channel_id=1, source_target_pairs={{0,1},{1,2},{2,3},{3,4},{4,5},{5,6},{6,7},{7,8},{8,9},{9,10},{10,1... | collective-permute-start | bytes 3080 | tf_op jit(solution)/shard_map/ppermute | solution.py:30
  156.8 4.6 %collective-permute-start.4 = (f32[1,256]{1,0:T(1,128)S(1)}, f32[1,256]{1,0:T(1,128)S(1)}, u32[]{:S(2)}, u32[]{:S(2)}) collective-permute-start(f32[1,256]{1,0:T(1,128)S(1)} %get-tuple-element.46), channel_id=1, source_target_pairs={{1,0},{2,1},{3,2},{4,3},{5,4},{6,5},{7,6},{8,7},{9,8},{10,9},{11,1... | collective-permute-start | bytes 3080 | tf_op jit(solution)/shard_map/ppermute | solution.py:33
  158.2 3.8 %collective-permute-start.5 = (f32[1,256]{1,0:T(1,128)S(1)}, f32[1,256]{1,0:T(1,128)S(1)}, u32[]{:S(2)}, u32[]{:S(2)}) collective-permute-start(f32[1,256]{1,0:T(1,128)S(1)} %get-tuple-element.47), channel_id=1, source_target_pairs={{0,1},{1,2},{2,3},{3,4},{4,5},{5,6},{6,7},{7,8},{8,9},{9,10},{10,1... | collective-permute-start | bytes 3080 | tf_op jit(solution)/shard_map/ppermute | solution.py:30
  227.3 4.6 %collective-permute-start.6 = (f32[1,256]{1,0:T(1,128)S(1)}, f32[1,256]{1,0:T(1,128)S(1)}, u32[]{:S(2)}, u32[]{:S(2)}) collective-permute-start(f32[1,256]{1,0:T(1,128)S(1)} %get-tuple-element.44), channel_id=1, source_target_pairs={{1,0},{2,1},{3,2},{4,3},{5,4},{6,5},{7,6},{8,7},{9,8},{10,9},{11,1... | collective-permute-start | bytes 3080 | tf_op jit(solution)/shard_map/ppermute | solution.py:33
  228.7 3.8 %collective-permute-start.7 = (f32[1,256]{1,0:T(1,128)S(1)}, f32[1,256]{1,0:T(1,128)S(1)}, u32[]{:S(2)}, u32[]{:S(2)}) collective-permute-start(f32[1,256]{1,0:T(1,128)S(1)} %get-tuple-element.45), channel_id=1, source_target_pairs={{0,1},{1,2},{2,3},{3,4},{4,5},{5,6},{6,7},{7,8},{8,9},{9,10},{10,1... | collective-permute-start | bytes 3080 | tf_op jit(solution)/shard_map/ppermute | solution.py:30
  238.3 46.3 %copy-start.8 = (f32[16,16,512]{2,1,0:T(8,128)S(1)}, f32[16,16,512]{2,1,0:T(8,128)}, u32[]{:S(2)}) copy-start(f32[16,16,512]{2,1,0:T(8,128)} %param.16) | copy-start | bytes 1572868
  270.9 16.8 %copy-start.12 = (f32[32,256]{1,0:T(8,128)}, f32[32,256]{1,0:T(8,128)S(1)}, u32[]{:S(2)}) copy-start(f32[32,256]{1,0:T(8,128)S(1)} %multiply_add_fusion) | copy-start | bytes 98308
  272.1 10.4 %all-to-all-start = ((f32[16,1,1024]{2,1,0:T(1,128)}), f32[16,1,1024]{2,1,0:T(1,128)S(1)}, u32[]{:S(2)}, u32[]{:S(2)}) async-start(f32[16,1,1024]{2,1,0:T(1,128)} %reshape.32), calls=%async_computation | async-start | bytes 131072 | tf_op jit(solution)/shard_map/all_to_all | solution.py:155
  284.3 8.0 %copy-start.14 = (s32[16,512]{1,0:T(8,128)S(1)}, s32[16,512]{1,0:T(8,128)}, u32[]{:S(2)}) copy-start(s32[16,512]{1,0:T(8,128)} %param.13) | copy-start | bytes 98308
  285.0 8.7 %copy-start.1 = (f32[8,16,16,512]{3,1,2,0:T(8,128)S(1)}, f32[8,16,16,512]{3,1,2,0:T(8,128)}, u32[]{:S(2)}) copy-start(f32[8,16,16,512]{3,1,2,0:T(8,128)} %copy-done) | copy-start | bytes 12582916
  285.1 8.7 %copy-start.2 = (f32[8,15,16,512]{3,1,2,0:T(8,128)S(1)}, f32[8,15,16,512]{3,1,2,0:T(8,128)}, u32[]{:S(2)}) copy-start(f32[8,15,16,512]{3,1,2,0:T(8,128)} %slice.315) | copy-start | bytes 11796484
  287.7 13.1 %collective-permute-start.8 = (f32[10,16,2,512]{3,1,2,0:T(8,128)}, f32[10,16,2,512]{3,1,2,0:T(8,128)}, u32[]{:S(2)}, u32[]{:S(2)}) collective-permute-start(f32[10,16,2,512]{3,1,2,0:T(8,128)} %get-tuple-element.29), channel_id=1, source_target_pairs={{0,1},{1,2},{2,3},{3,4},{4,5},{5,6},{6,7},{7,8},{8,9},{9,10},{10,1... | collective-permute-start | bytes 1966088 | tf_op jit(solution)/shard_map/ppermute | solution.py:30
  287.7 14.1 %collective-permute-start.9 = (f32[10,16,2,512]{3,1,2,0:T(8,128)}, f32[10,16,2,512]{3,1,2,0:T(8,128)}, u32[]{:S(2)}, u32[]{:S(2)}) collective-permute-start(f32[10,16,2,512]{3,1,2,0:T(8,128)} %get-tuple-element.30), channel_id=1, source_target_pairs={{1,0},{2,1},{3,2},{4,3},{5,4},{6,5},{7,6},{8,7},{9,8},{10,9},{11,1... | collective-permute-start | bytes 1966088 | tf_op jit(solution)/shard_map/ppermute | solution.py:33
  293.8 3.8 %copy-start.9 = (f32[16,16,512]{2,1,0:T(8,128)S(1)}, f32[16,16,512]{2,1,0:T(8,128)}, u32[]{:S(2)}) copy-start(f32[16,16,512]{2,1,0:T(8,128)} %param.16) | copy-start | bytes 1572868
  293.8 7.8 %copy-start.7 = (f32[16,16,512]{2,0,1:T(8,128)S(1)}, f32[16,16,512]{2,0,1:T(8,128)}, u32[]{:S(2)}) copy-start(f32[16,16,512]{2,0,1:T(8,128)} %fusion.19) | copy-start | bytes 1572868
  293.8 8.0 %copy-start.6 = (f32[1,16,16,512]{3,1,2,0:T(8,128)S(1)}, f32[1,16,16,512]{3,1,2,0:T(8,128)}, u32[]{:S(2)}) copy-start(f32[1,16,16,512]{3,1,2,0:T(8,128)} %copy-done.5) | copy-start | bytes 1572868
where the time goes:
time: 333 us; the launch traced here: 329 us
  blocking collectives  220 us (66%)
  other arithmetic  46.5 us (14%)
  starting transfers between devices  24.5 us (7%)
  local copies, waits for them, and re-layouts  16.6 us (5%)
  waiting for transfers between devices  10.6 us (3%)
  between operations  10.4 us (3%)
    psum x4, blocking collectives, squared_total(): return lax.psum(jnp.sum(residual * residual), 'lon')  127 us
    psum x3, blocking collectives, plain_solve(): curvature = lax.psum(jnp.sum(direction * applied), 'lon')  93.4 us
    add x1, other arithmetic, body(): tracers_new = tracers + wet[None] * tendency  11.7 us
    ppermute x5, starting transfers between devices, padded_2(): lax.ppermute(lax.slice_in_dim(block, block.shape[dim] - width, None, axis...  11.4 us
    ppermute x5, starting transfers between devices, padded_2(): lax.ppermute(lax.slice_in_dim(block, 0, width, axis=dim), axis, backward)  9.59 us
    unnamed x33, local copies, waits for them, and re-layouts  7.77 us
  transfers between devices with their start and end apart: 11, of which 5 were waited for; matrix products, arithmetic and copies ran while one was open for 5% of the time, Pallas kernels for 0%

commit v1 on v0

--- a/solution.py
+++ b/solution.py
@@ -20,28 +20,36 @@
 YIELD_NITROUS = 0.3
 
 
-def padded_2(block, sides, width, periodic):
-    for axis, dim in sides:
-        count = lax.axis_size(axis)
-        forward = [(i, i + 1) for i in range(count - 1)]
-        if periodic:
-            forward.append((count - 1, 0))
-        backward = [(target, source) for source, target in forward]
-        low = lax.ppermute(
-            lax.slice_in_dim(block, block.shape[dim] - width, None, axis=dim), axis, forward
-        )
-        high = lax.ppermute(lax.slice_in_dim(block, 0, width, axis=dim), axis, backward)
-        block = jnp.concatenate([low, block, high], axis=dim)
-    return block
-
-
-def apply_operator(values_in, mask_float, coeff):
+def padded_2(block, width):
+    low = shifted(block[:, :, -width:], "lon", 1, True)
+    high = shifted(block[:, :, :width], "lon", -1, True)
+    return low, high
+
+
+HALO = SOLVER_ITERS
+CENTER = 4.55
+HALF_WIDTH = 4.45
+
+
+def shifted(block, axis_name, step, periodic):
+    count = lax.axis_size(axis_name)
+    pairs = [(i, (i + step) % count) for i in range(count) if periodic or 0 <= i + step < count]
+    return lax.ppermute(block, axis_name, pairs)
+
+
+def extended_band(fields):
+    below = shifted(fields[:, -HALO:], "lon", 1, False)
+    above = shifted(fields[:, :HALO], "lon", -1, False)
+    top_device = lax.axis_index("lon") == lax.axis_size("lon") - 1
+    above = jnp.where(top_device, fields[:, -HALO:][:, ::-1, ::-1], above)
+    return jnp.concatenate([below, fields, above], axis=1)
+
+
+def apply_extended(values_in, mask_float, coeff):
     masked = mask_float * values_in
-    padded = padded_2(masked, (("lon", 0),), 1, False)
-    top_device = lax.axis_index("lon") == lax.axis_size("lon") - 1
-    folded = jnp.where(top_device, masked[-1:, ::-1], padded[-1:])
-    northern = jnp.concatenate([padded[2:-1], folded], axis=0)
-    southern = padded[:-2]
+    edge = jnp.zeros_like(masked[:1])
+    northern = jnp.concatenate([masked[1:], edge], axis=0)
+    southern = jnp.concatenate([edge, masked[:-1]], axis=0)
     eastern = jnp.roll(masked, -1, axis=1)
     western = jnp.roll(masked, 1, axis=1)
     return (coeff + 4.0 * mask_float) * values_in - mask_float * (
@@ -49,25 +57,96 @@
     )
 
 
-def squared_total(residual):
-    return lax.psum(jnp.sum(residual * residual), "lon")
-
-
-def plain_solve(right_side, mask_float, coeff):
-    solution = jnp.zeros_like(right_side)
-    residual = right_side
-    direction = right_side
-    norm_now = squared_total(residual)
+def krylov_basis(extended):
+    right_side, coeff, mask_float = extended[0], extended[1], extended[2]
+    basis = [right_side]
+    for order in range(SOLVER_ITERS):
+        now = basis[-1]
+        image = (apply_extended(now, mask_float, coeff) - CENTER * now) * (1.0 / HALF_WIDTH)
+        basis.append(image if order == 0 else 2.0 * image - basis[-2])
+    return [field[HALO:-HALO] for field in basis]
+
+
+GRAM_PAIRS = [(i, j) for i in range(SOLVER_ITERS) for j in range(i, SOLVER_ITERS + 1)]
+
+
+def operator_on_coefficients(given):
+    out = [CENTER * value for value in given] + [0.0]
+    for k, value in enumerate(given):
+        if k == 0:
+            out[1] = out[1] + HALF_WIDTH * value
+        else:
+            out[k - 1] = out[k - 1] + 0.5 * HALF_WIDTH * value
+            out[k + 1] = out[k + 1] + 0.5 * HALF_WIDTH * value
+    return out
+
+
+def gram_product(gram, left, right):
+    total = 0.0
+    for i, x in enumerate(left):
+        for j, y in enumerate(right):
+            total = total + gram[(min(i, j), max(i, j))] * (x * y)
+    return total
+
+
+def added(first, second):
+    size = max(len(first), len(second))
+    first = list(first) + [0.0] * (size - len(first))
+    second = list(second) + [0.0] * (size - len(second))
+    return [x + y for x, y in zip(first, second)]
+
+
+def solver_coefficients(gram):
+    one = jnp.ones_like(gram[(0, 0)])
+    solution, residual, direction = [], [one], [one]
+    norm_now = gram[(0, 0)]
     for sweep in range(SOLVER_ITERS):
-        applied = apply_operator(direction, mask_float, coeff)
-        curvature = lax.psum(jnp.sum(direction * applied), "lon")
-        step_size = norm_now / curvature
-        solution = solution + step_size * direction
-        residual = residual - step_size * applied
-        norm_next = squared_total(residual)
-        direction = residual + norm_next / norm_now * direction
+        applied = operator_on_coefficients(direction)
+        step_size = norm_now / gram_product(gram, direction, applied)
+        solution = added(solution, [step_size * x for x in direction])
+        if sweep == SOLVER_ITERS - 1:
+            break
+        residual = added(residual, [-step_size * x for x in applied])
+        norm_next = gram_product(gram, residual, residual)
+        ratio = norm_next / norm_now
+        direction = added(residual, [ratio * x for x in direction])
         norm_now = norm_next
     return solution
+
+
+def solve_and_hand_over(surface_old, surface_forcing, surface_coeff, ocean_mask):
+    rows, columns = surface_old.shape
+    count = lax.axis_size("lon")
+    width = columns // count
+    right_side = surface_coeff * surface_old + surface_forcing
+    extended = extended_band(
+        jnp.stack([right_side, surface_coeff, ocean_mask.astype(jnp.float32)])
+    )
+    basis = krylov_basis(extended)
+    partial = jnp.stack([jnp.sum(basis[i] * basis[j]) for i, j in GRAM_PAIRS])
+    stacked = jnp.stack(basis[:SOLVER_ITERS])
+    parts = stacked.reshape(SOLVER_ITERS, rows, count, width)
+    west = jnp.roll(parts[..., -1:], 1, axis=2)
+    east = jnp.roll(parts[..., :1], -1, axis=2)
+    wide = jnp.concatenate([west, parts, east], axis=-1)
+    wide = wide.transpose(2, 3, 0, 1).reshape(count, width + 2, SOLVER_ITERS * rows)
+    lanes = max(wide.shape[2], 128)
+    wide = jnp.pad(wide, ((0, 0), (0, 0), (0, lanes - wide.shape[2])))
+    sums = jnp.broadcast_to(
+        jnp.pad(partial, (0, lanes - len(GRAM_PAIRS)))[None, None], (count, 1, lanes)
+    )
+    moved = lax.all_to_all(
+        jnp.concatenate([wide, sums], axis=1), "lon", split_axis=0, concat_axis=0, tiled=True
+    )
+    totals = jnp.sum(moved[:, width + 2], axis=0)
+    gram = {pair: totals[n] for n, pair in enumerate(GRAM_PAIRS)}
+    weights = solver_coefficients(gram)
+    surface = sum(weights[k] * basis[k] for k in range(SOLVER_ITERS))
+    strip = sum(
+        weights[k] * moved[:, : width + 2, k * rows : (k + 1) * rows] for k in range(SOLVER_ITERS)
+    )
+    strip = strip.transpose(1, 0, 2).reshape(width + 2, count * rows)
+    return surface, strip
 
 
 def open_faces(column_depth, east_depth, east_baro, north_baro, u_clinic, v_clinic):
@@ -148,28 +227,24 @@
     u_clinic,
     v_clinic,
 ):
-    mask_float = ocean_mask.astype(jnp.float32)
-    right_side = surface_coeff * surface_old + surface_forcing
-    surface = plain_solve(right_side, mask_float, surface_coeff)
-    band_flow = -BARO_GAIN * (jnp.roll(surface, -1, axis=1) - surface)
-    moved = lax.all_to_all(
-        jnp.stack([surface, band_flow]), "lon", split_axis=2, concat_axis=1, tiled=True
-    )
-    strip_surface = moved[0].T
-    east_baro = moved[1].T
+    surface, wide_strip = solve_and_hand_over(
+        surface_old, surface_forcing, surface_coeff, ocean_mask
+    )
+    strip_surface = wide_strip[1:-1]
+    wide_baro = -BARO_GAIN * (wide_strip[1:] - wide_strip[:-1])
+    east_baro = wide_baro[1:]
     above_surface = jnp.concatenate([strip_surface[:, 1:], strip_surface[:, -1:]], axis=1)
     north_baro = -BARO_GAIN * (above_surface - strip_surface)
     wet, east_open, north_open, below_open, east_flow, north_flow = open_faces(
         column_depth, east_depth, east_baro, north_baro, u_clinic, v_clinic
     )
     masked = tracers * wet[None]
-    tracer_count = masked.shape[0]
     columns_here = masked.shape[2]
-    stacked = jnp.concatenate([masked, east_flow[None], east_open[None]], axis=0)
-    padded = padded_2(stacked, (("lon", 2),), 2, True)
-    tracer_pad = padded[:tracer_count]
-    west_flow = padded[tracer_count, :, 1:2]
-    west_open = padded[tracer_count + 1, :, 1:2]
+    low, high = padded_2(masked, 2)
+    tracer_pad = jnp.concatenate([low, masked, high], axis=2)
+    west_u = shifted(u_clinic[:, -1:], "lon", 1, True)
+    west_open = shifted(east_open[:, -1:], "lon", 1, True)
+    west_flow = (west_u + wide_baro[None, :1]) * west_open
     flow_all = jnp.concatenate([west_flow, east_flow], axis=1)
     open_all = jnp.concatenate([west_open, east_open], axis=1)
     center = tracer_pad[:, :, 1 : columns_here + 2]

time: 333 us -> 135 us (0.41)
  blocking collectives: 220 us -> 0 us
  between operations: 10.4 us -> 39.5 us
  local copies, waits for them, and re-layouts: 16.6 us -> 31.1 us
  waiting for transfers between devices: 10.6 us -> 0.28 us
  starting transfers between devices: 24.5 us -> 15.6 us
    psum x7 -> x0, blocking collectives: 220 us -> none  [the longest x4 127 us: squared_total(): return lax.psum(jnp.sum(residual * residual), 'lon')]
    ppermute x10 -> x6, starting transfers between devices: 21 us -> 11.9 us  [shifted(): return lax.ppermute(block, axis_name, pairs)]
    another operation x1 -> x2, local copies, waits for them, and re-layouts: 0.15 us -> 8.71 us  [the longest x1 8.65 us: solve_and_hand_over(): partial = jnp.stack([jnp.sum(basis[i] * basis[j]) for i, j in GRAM_PAIRS])]
    all_to_all x1, waiting for transfers between devices: 5.99 us -> 0.26 us  [solve_and_hand_over(): lax.all_to_all(jnp.concatenate([wide, sums], axis=1), 'lon', split_axis=0...]
    unnamed x7, other arithmetic: 1.76 us -> 7.27 us
    ppermute x10 -> x6, waiting for transfers between devices: 4.6 us -> 0.02 us  [shifted(): return lax.ppermute(block, axis_name, pairs)]
    concatenate x1 -> x2, other arithmetic: 4.39 us -> 0.03 us  [the longest x1 0.02 us: extended_band(): return jnp.concatenate([below, fields, above], axis=1)]
    reduce_sum x7 -> x2, other arithmetic: 4.73 us -> 1.07 us  [the longest x1 1.03 us: solve_and_hand_over(): partial = jnp.stack([jnp.sum(basis[i] * basis[j]) for i, j in GRAM_PAIRS])]
  transfers between devices with their start and end apart: 11 -> 7, of which waited for: 5 -> 1; matrix products, arithmetic and copies ran while one was open for 5% -> 39% of each run, Pallas kernels for 0% -> 0%
where the time goes in v1:
time: 135 us; the launch traced here: 133 us
  other arithmetic  46.6 us (35%)
  between operations  39.5 us (29%)
  local copies, waits for them, and re-layouts  31.1 us (23%)
  starting transfers between devices  15.6 us (12%)
    ppermute x6, starting transfers between devices, shifted(): return lax.ppermute(block, axis_name, pairs)  11.9 us
    add x1, other arithmetic, body(): tracers_new = tracers + wet[None] * tendency  11.9 us
    unnamed x23, local copies, waits for them, and re-layouts  10.8 us
    another operation x1, local copies, waits for them, and re-layouts, solve_and_hand_over(): partial = jnp.stack([jnp.sum(basis[i] * basis[j]) for i, j in GRAM_PAIRS])  8.65 us
    unnamed x7, other arithmetic  7.27 us
    sub x1, other arithmetic, meridional_vertical(): north_flow * face_north - HORIZ_DIFF * (north_one - masked) * north_open  5.36 us
    slice x1, local copies, waits for them, and re-layouts, meridional_vertical(): masked[..., 1:, :, :]  5.04 us
    mul x1, other arithmetic, body(): masked = tracers * wet[None]  4.73 us
  transfers between devices with their start and end apart: 7, of which 1 were waited for; matrix products, arithmetic and copies ran while one was open for 39% of the time, Pallas kernels for 0%

profile of v1, /device:TPU:0, one launch (start us, length us, event | category | flops | bytes accessed | tf_op | source)
XLA Modules:
  0.0 133.1 jit_solution(15075009628388911102)
XLA Ops:
  0.6 0.9 copy.135
  1.5 0.9 copy.136
  2.3 0.9 copy.137
  3.3 0.8 convert_bitcast_fusion
  4.1 0.7 pad_maximum_fusion.16
  4.8 1.3 collective-permute-start.1
  6.1 3.0 %collective-permute-start = (f32[3,4,256]{2,1,0:T(4,128)S(1)}, f32[3,4,256]{2,1,0:T(4,128)S(1)}, u32[]{:S(2)}, u32[]{:S(2)}) collective-permute-start(f32[3,4,256]{2,1,0:T(4,128)S(1)} %get-tuple-element.72), channel_id=1, source_target_pairs={{0,1},{1,2},{2,3},{3,4},{4,5},{5,6},{6,7},{7,8},{8,9},{9,10},{10,1... | collective-permute-start | bytes 36872 | tf_op jit(solution)/shard_map/ppermute | solution.py:37
  9.1 0.8 fusion.26
  9.9 0.6 slice.438
  10.6 2.6 %collective-permute-start.5 = (f32[16,1,512]{2,0,1:T(8,128)}, f32[16,1,512]{2,0,1:T(8,128)}, u32[]{:S(2)}, u32[]{:S(2)}) collective-permute-start(f32[16,1,512]{2,0,1:T(8,128)} %slice.438), channel_id=1, source_target_pairs={{0,1},{1,2},{2,3},{3,4},{4,5},{5,6},{6,7},{7,8},{8,9},{9,10},{10,1... | collective-permute-start | bytes 98312 | tf_op jit(solution)/shard_map/ppermute | solution.py:37
  13.2 1.0 slice.430
  14.1 0.6 copy.164
  14.7 0.5 collective-permute-start.4
  15.2 0.8 fusion.27
  16.1 4.7 %copy_multiply_fusion = f32[8,16,16,512]{3,1,2,0:T(8,128)S(1)} fusion(f32[8,16,16,512]{3,2,1,0:T(8,128)} %param.15, f32[16,16,512]{2,0,1:T(8,128)S(1)} %fusion.27), kind=kLoop, calls=%fused_computation.25 | loop fusion | flops 1048576 | bytes 8912896 | tf_op jit(solution)/shard_map/mul | solution.py:241
  20.8 1.3 fusion.59
  22.1 2.0 %collective-permute-start.2 = (f32[8,16,2,512]{3,1,2,0:T(8,128)}, f32[8,16,2,512]{3,1,2,0:T(8,128)}, u32[]{:S(2)}, u32[]{:S(2)}) collective-permute-start(f32[8,16,2,512]{3,1,2,0:T(8,128)} %get-tuple-element.36), channel_id=1, source_target_pairs={{0,1},{1,2},{2,3},{3,4},{4,5},{5,6},{6,7},{7,8},{8,9},{9,10},{10,1... | collective-permute-start | bytes 1572872 | tf_op jit(solution)/shard_map/ppermute | solution.py:37
  24.1 1.2 subtract_dynamic-update-slice_fusion.3
  25.2 1.1 add_dynamic-update-slice_fusion
  26.3 1.2 subtract_dynamic-update-slice_fusion.2
  27.5 1.0 subtract_dynamic-update-slice_fusion.1
  28.5 0.8 multiply_dynamic-update-slice_fusion
  29.3 0.8 negate_dynamic-update-slice_fusion
  30.2 1.1 subtract_dynamic-update-slice_fusion
  31.3 0.2 rev.3
  31.5 2.5 %collective-permute-start.3 = (f32[8,16,2,512]{3,1,2,0:T(8,128)}, f32[8,16,2,512]{3,1,2,0:T(8,128)}, u32[]{:S(2)}, u32[]{:S(2)}) collective-permute-start(f32[8,16,2,512]{3,1,2,0:T(8,128)} %get-tuple-element.37), channel_id=1, source_target_pairs={{0,15},{1,0},{2,1},{3,2},{4,3},{5,4},{6,5},{7,6},{8,7},{9,8},{10,9... | collective-permute-start | bytes 1572872 | tf_op jit(solution)/shard_map/ppermute | solution.py:37
  35.6 1.0 multiply_reduce_fusion
  36.7 0.4 copy.142
  37.1 0.3 reshape.68
  37.4 8.6 %stack.106 = f32[14]{0:T(128)S(1)} concatenate(f32[1]{0:T(128)} %bitcast.11, f32[1]{0:T(128)} %bitcast.12, f32[1]{0:T(128)} %bitcast.13, f32[1]{0:T(128)} %bitcast.14, f32[1]{0:T(128)} %bitcast.15, f32[1]{0:T(128)} %bitcast.16, f32[1]{0:T(128)} %bitcast.17, f32[1]{0:T(128)} %bitcast.18, f32[1]{0:T(128)} %bitcast.19, f32[1]{0:T(128)} %bitcast.20, f32[1]{0:T(128)} %bitcast.21, ...), dimensions={0} | concatenate | bytes 112 | tf_op jit(solution)/shard_map/stack | solution.py:126
  46.1 0.7 copy.143
  46.9 3.7 %all-to-all-start = ((f32[16,19,128]{2,1,0:T(8,128)}), f32[16,19,128]{2,1,0:T(8,128)S(1)}, u32[]{:S(2)}, u32[]{:S(2)}) async-start(f32[16,19,128]{2,1,0:T(8,128)} %copy.143), calls=%async_computation | async-start | bytes 393216 | tf_op jit(solution)/shard_map/all_to_all | solution.py:138
  50.6 2.4 %fusion.21 = f32[8,16,16,512]{3,1,2,0:T(8,128)} fusion(f32[8,16,16,512]{3,1,2,0:T(8,128)} %subtract_dynamic-update-slice_fusion, f32[8,16,16,512]{3,1,2,0:T(8,128)} %copy-done), kind=kLoop, calls=%fused_computation.49 | loop fusion | flops 1179648 | bytes 2097152 | tf_op jit(solution)/shard_map/stack | solution.py:199
  52.9 0.2 slice.445
  53.2 5.0 %slice.447 = f32[8,15,16,512]{3,1,2,0:T(8,128)} slice(f32[8,16,16,512]{3,1,2,0:T(8,128)} %copy-done), slice={[0:8], [1:16], [0:16], [0:512]} | slice | bytes 7864320 | tf_op jit(solution)/shard_map/slice | solution.py:175
  58.2 0.8 maximum_multiply_fusion.1
  59.1 0.3 all-to-all-done
  59.4 0.7 fusion.73
  98.5 0.2 fusion.31
  99.1 1.1 multiply_add_fusion
  100.4 1.4 %add_select_fusion = f32[16,16,512]{2,0,1:T(8,128)S(1)} fusion(f32[16,512]{1,0:T(8,128)S(1)} %slice.364, s32[16,512]{1,0:T(8,128)S(1)} %copy-done.6, f32[16,16,512]{2,1,0:T(8,128)} %param.16), kind=kLoop, calls=%fused_computation.69 | loop fusion | flops 393216 | bytes 1114112 | tf_op jit(solution)/shard_map/mul | solution.py:158
  102.0 0.7 copy.151
  102.7 0.9 add_multiply_fusion
  103.7 1.8 %fusion.25 = (f32[16,16,512]{2,0,1:T(8,128)S(1)}, f32[16,16,512]{2,0,1:T(8,128)S(1)}, f32[16,16,512]{2,0,1:T(8,128)S(1)}) fusion(f32[16,16,512]{2,1,0:T(8,128)} %param.17, f32[16,16,511]{2,0,1:T(8,128)S(1)} %slice.445, f32[16,512]{1,0:T(8,128)S(1)} %fusion.55, s32[16,512]{1,0:T(8,128)S(1)} %copy-done.5, f32[15,16,512]{2,0,1:T(8,128)S(1)} %slice.448), kind=kLoop, calls=%fused_computation.56 | loop fusion | flops 1048576 | bytes 3177472 | tf_op jit(solution)/shard_map/mul | solution.py:171
  105.5 5.4 %fusion.9 = (f32[8,16,16,512]{3,1,2,0:T(8,128)S(1)}, f32[8,16,16,512]{3,1,2,0:T(8,128)S(1)}) fusion(f32[8,16,16,512]{3,1,2,0:T(8,128)S(1)} %copy-done.1, f32[16,16,512]{2,0,1:T(8,128)S(1)} %get-tuple-element.39, f32[16,16,512]{2,0,1:T(8,128)S(1)} %get-tuple-element.38, f32[16,16,512]{2,0,1:T(8,128)S(1)} %get-tuple-element.73, f32[8,15,16,512]{3,1,2,0:T(8,128)} %slice.447), kind=kLoop, calls=%fused_computation.18 | loop fusion | flops 10485760 | bytes 18087936 | tf_op jit(solution)/shard_map/sub | solution.py:171
  110.9 3.6 %fusion.5 = f32[8,16,17,512]{3,1,2,0:T(8,128)S(1)} fusion(f32[8,16,2,512]{3,1,2,0:T(8,128)} %collective-permute-done.3, f32[8,16,16,512]{3,1,2,0:T(8,128)S(1)} %copy-done.1, f32[8,16,2,512]{3,1,2,0:T(8,128)} %collective-permute-done.2, f32[16,17,512]{2,0,1:T(8,128)S(1)} %maximum_multiply_fusion.1, f32[16,17,512]{2,0,1:T(8,128)S(1)} %maximum_multiply_fusion), kind=kLoop, calls=%fused_computation.13 | loop fusion | flops 13369344 | bytes 10813440 | tf_op jit(solution)/shard_map/sub | solution.py:255
  114.5 11.9 %fusion.13 = f32[8,16,16,512]{3,1,2,0:T(8,128)} fusion(f32[8,16,16,512]{3,1,2,0:T(8,128)} %fusion.21, f32[8,16,17,512]{3,1,2,0:T(8,128)S(1)} %fusion.5, f32[8,16,16,512]{3,1,2,0:T(8,128)S(1)} %get-tuple-element.35, f32[8,15,16,512]{3,1,2,0:T(8,128)S(1)} %bitcast.85, f32[8,16,16,512]{3,1,2,0:T(8,128)S(1)} %get-tuple-element.34, ...), kind=kLoop, calls=%fused_computation.23 | loop fusion | flops 8388608 | bytes 38002688 | tf_op jit(solution)/shard_map/add | solution.py:261
  126.4 6.7 %copy.152 = f32[8,16,16,512]{3,2,1,0:T(8,128)} copy(f32[8,16,16,512]{3,1,2,0:T(8,128)} %fusion.13) | data formatting | bytes 8388608
  (65 shorter events, 2.4 us)
Async XLA Ops:
  4.8 26.7 %collective-permute-start.1 = (f32[3,4,256]{2,1,0:T(4,128)S(1)}, f32[3,4,256]{2,1,0:T(4,128)S(1)}, u32[]{:S(2)}, u32[]{:S(2)}) collective-permute-start(f32[3,4,256]{2,1,0:T(4,128)S(1)} %get-tuple-element.71), channel_id=1, source_target_pairs={{1,0},{2,1},{3,2},{4,3},{5,4},{6,5},{7,6},{8,7},{9,8},{10,9},{11,1... | collective-permute-start | bytes 36872 | tf_op jit(solution)/shard_map/ppermute | solution.py:37
  6.1 28.0 %collective-permute-start = (f32[3,4,256]{2,1,0:T(4,128)S(1)}, f32[3,4,256]{2,1,0:T(4,128)S(1)}, u32[]{:S(2)}, u32[]{:S(2)}) collective-permute-start(f32[3,4,256]{2,1,0:T(4,128)S(1)} %get-tuple-element.72), channel_id=1, source_target_pairs={{0,1},{1,2},{2,3},{3,4},{4,5},{5,6},{6,7},{7,8},{8,9},{9,10},{10,1... | collective-permute-start | bytes 36872 | tf_op jit(solution)/shard_map/ppermute | solution.py:37
  10.6 47.7 %collective-permute-start.5 = (f32[16,1,512]{2,0,1:T(8,128)}, f32[16,1,512]{2,0,1:T(8,128)}, u32[]{:S(2)}, u32[]{:S(2)}) collective-permute-start(f32[16,1,512]{2,0,1:T(8,128)} %slice.438), channel_id=1, source_target_pairs={{0,1},{1,2},{2,3},{3,4},{4,5},{5,6},{6,7},{7,8},{8,9},{9,10},{10,1... | collective-permute-start | bytes 98312 | tf_op jit(solution)/shard_map/ppermute | solution.py:37
  14.7 88.0 %collective-permute-start.4 = (f32[16,1,512]{2,0,1:T(8,128)}, f32[16,1,512]{2,0,1:T(8,128)}, u32[]{:S(2)}, u32[]{:S(2)}) collective-permute-start(f32[16,1,512]{2,0,1:T(8,128)} %copy.164), channel_id=1, source_target_pairs={{0,1},{1,2},{2,3},{3,4},{4,5},{5,6},{6,7},{7,8},{8,9},{9,10},{10,1... | collective-permute-start | bytes 98312 | tf_op jit(solution)/shard_map/ppermute | solution.py:37
  20.8 9.4 %copy-start = (f32[8,16,16,512]{3,1,2,0:T(8,128)}, f32[8,16,16,512]{3,1,2,0:T(8,128)S(1)}, u32[]{:S(2)}) copy-start(f32[8,16,16,512]{3,1,2,0:T(8,128)S(1)} %copy_multiply_fusion) | copy-start | bytes 12582916
  22.1 88.8 %collective-permute-start.2 = (f32[8,16,2,512]{3,1,2,0:T(8,128)}, f32[8,16,2,512]{3,1,2,0:T(8,128)}, u32[]{:S(2)}, u32[]{:S(2)}) collective-permute-start(f32[8,16,2,512]{3,1,2,0:T(8,128)} %get-tuple-element.36), channel_id=1, source_target_pairs={{0,1},{1,2},{2,3},{3,4},{4,5},{5,6},{6,7},{7,8},{8,9},{9,10},{10,1... | collective-permute-start | bytes 1572872 | tf_op jit(solution)/shard_map/ppermute | solution.py:37
  27.5 6.6 %copy-start.4 = (f32[32,256]{1,0:T(8,128)S(1)}, f32[32,256]{1,0:T(8,128)}, u32[]{:S(2)}) copy-start(f32[32,256]{1,0:T(8,128)} %param.11) | copy-start | bytes 98308
  31.5 79.4 %collective-permute-start.3 = (f32[8,16,2,512]{3,1,2,0:T(8,128)}, f32[8,16,2,512]{3,1,2,0:T(8,128)}, u32[]{:S(2)}, u32[]{:S(2)}) collective-permute-start(f32[8,16,2,512]{3,1,2,0:T(8,128)} %get-tuple-element.37), channel_id=1, source_target_pairs={{0,15},{1,0},{2,1},{3,2},{4,3},{5,4},{6,5},{7,6},{8,7},{9,8},{10,9... | collective-permute-start | bytes 1572872 | tf_op jit(solution)/shard_map/ppermute | solution.py:37
  34.7 1.9 %copy-start.3 = (f32[40,256]{0,1:T(8,128)}, f32[40,256]{0,1:T(8,128)S(1)}, u32[]{:S(2)}) copy-start(f32[40,256]{0,1:T(8,128)S(1)} %get-tuple-element.28) | copy-start | bytes 122884
  35.3 1.3 copy-start.2
  46.9 12.5 %all-to-all-start = ((f32[16,19,128]{2,1,0:T(8,128)}), f32[16,19,128]{2,1,0:T(8,128)S(1)}, u32[]{:S(2)}, u32[]{:S(2)}) async-start(f32[16,19,128]{2,1,0:T(8,128)} %copy.143), calls=%async_computation | async-start | bytes 393216 | tf_op jit(solution)/shard_map/all_to_all | solution.py:138
  58.2 42.2 %copy-start.6 = (s32[16,512]{1,0:T(8,128)S(1)}, s32[16,512]{1,0:T(8,128)}, u32[]{:S(2)}) copy-start(s32[16,512]{1,0:T(8,128)} %param.14) | copy-start | bytes 98308
  58.2 45.5 %copy-start.5 = (s32[16,512]{1,0:T(8,128)S(1)}, s32[16,512]{1,0:T(8,128)}, u32[]{:S(2)}) copy-start(s32[16,512]{1,0:T(8,128)} %param.13) | copy-start | bytes 98308
  102.7 2.8 %copy-start.1 = (f32[8,16,16,512]{3,1,2,0:T(8,128)S(1)}, f32[8,16,16,512]{3,1,2,0:T(8,128)}, u32[]{:S(2)}) copy-start(f32[8,16,16,512]{3,1,2,0:T(8,128)} %copy-done) | copy-start | bytes 12582916

commit v2 on v1

--- a/solution.py
+++ b/solution.py
@@ -1,9 +1,12 @@
 import jax
 import jax.numpy as jnp
 from jax import lax
+from jax.experimental import pallas as pl
+from jax.experimental.pallas import tpu as pltpu
 from jax.sharding import PartitionSpec as P
 
 SOLVER_ITERS = 4
+TRACERS = 8
 
 
 BARO_GAIN = 0.1
@@ -20,15 +23,13 @@
 YIELD_NITROUS = 0.3
 
 
-def padded_2(block, width):
-    low = shifted(block[:, :, -width:], "lon", 1, True)
-    high = shifted(block[:, :, :width], "lon", -1, True)
-    return low, high
-
-
 HALO = SOLVER_ITERS
 CENTER = 4.55
 HALF_WIDTH = 4.45
+LANES = 128
+RING = 24
+WIDTH = 16
+SUM_ROW = WIDTH + 1
 
 
 def shifted(block, axis_name, step, periodic):
@@ -97,7 +98,7 @@
 
 
 def solver_coefficients(gram):
-    one = jnp.ones_like(gram[(0, 0)])
+    one = gram[(0, 0)] * 0.0 + 1.0
     solution, residual, direction = [], [one], [one]
     norm_now = gram[(0, 0)]
     for sweep in range(SOLVER_ITERS):
@@ -130,54 +131,47 @@
     east = jnp.roll(parts[..., :1], -1, axis=2)
     wide = jnp.concatenate([west, parts, east], axis=-1)
     wide = wide.transpose(2, 3, 0, 1).reshape(count, width + 2, SOLVER_ITERS * rows)
-    lanes = max(wide.shape[2], 128)
-    wide = jnp.pad(wide, ((0, 0), (0, 0), (0, lanes - wide.shape[2])))
+    wide = jnp.tile(wide, (1, 1, LANES // wide.shape[2]))
     sums = jnp.broadcast_to(
-        jnp.pad(partial, (0, lanes - len(GRAM_PAIRS)))[None, None], (count, 1, lanes)
-    )
-    moved = lax.all_to_all(
-        jnp.concatenate([wide, sums], axis=1), "lon", split_axis=0, concat_axis=0, tiled=True
-    )
-    totals = jnp.sum(moved[:, width + 2], axis=0)
-    gram = {pair: totals[n] for n, pair in enumerate(GRAM_PAIRS)}
+        jnp.pad(partial, (0, LANES - len(GRAM_PAIRS)))[None, None], (count, 1, LANES)
+    )
+    spare = jnp.zeros((count, RING - width - 3, LANES), jnp.float32)
+    payload = jnp.concatenate([wide[:, 1:], sums, spare, wide[:, :1]], axis=1)
+    moved = lax.all_to_all(payload, "lon", split_axis=0, concat_axis=0, tiled=True)
+    return pl.pallas_call(
+        combine_kernel,
+        out_shape=(
+            jax.ShapeDtypeStruct((rows, columns), jnp.float32),
+            jax.ShapeDtypeStruct((RING, rows * count), jnp.float32),
+        ),
+    )(moved, stacked)
+
+
+def combine(moved, basis, surface_ref, strip_ref):
+    count, rows = moved.shape[0], basis.shape[1]
+    totals = jnp.sum(moved[:, SUM_ROW : SUM_ROW + 1, :], axis=0)
+    gram = {pair: totals[:, n : n + 1] for n, pair in enumerate(GRAM_PAIRS)}
     weights = solver_coefficients(gram)
-    surface = sum(weights[k] * basis[k] for k in range(SOLVER_ITERS))
-    strip = sum(
-        weights[k] * moved[:, : width + 2, k * rows : (k + 1) * rows] for k in range(SOLVER_ITERS)
-    )
-    strip = strip.transpose(1, 0, 2).reshape(width + 2, count * rows)
-    return surface, strip
-
-
-def open_faces(column_depth, east_depth, east_baro, north_baro, u_clinic, v_clinic):
-    level_index = lax.broadcasted_iota(jnp.int32, u_clinic.shape, 0)
-    wet = (level_index < column_depth[None]).astype(jnp.float32)
-    east_open = (level_index < east_depth[None]).astype(jnp.float32)
-    north_open = wet * jnp.concatenate([wet[:, :, 1:], jnp.zeros_like(wet[:, :, :1])], axis=2)
-    below_open = wet * jnp.concatenate([wet[1:], jnp.zeros_like(wet[:1])], axis=0)
-    east_flow = (u_clinic + east_baro[None]) * east_open
-    north_flow = (v_clinic + north_baro[None]) * north_open
-    return (wet, east_open, north_open, below_open, east_flow, north_flow)
-
-
-def meridional_vertical(masked, north_flow, north_open, below_open):
-    count_rows = masked.shape[-1]
-    pad_widths = [(0, 0)] * (masked.ndim - 1) + [(2, 2)]
-    padded = jnp.pad(masked, pad_widths)
-    south_one = padded[..., 1 : count_rows + 1]
-    north_one = padded[..., 3 : count_rows + 3]
-    north_two = padded[..., 4 : count_rows + 4]
-    face_north = (7.0 * (masked + north_one) - (south_one + north_two)) / 12.0
-    flux_north = north_flow * face_north - HORIZ_DIFF * (north_one - masked) * north_open
-    flux_south = jnp.concatenate(
-        [jnp.zeros_like(flux_north[..., :1]), flux_north[..., :-1]], axis=-1
-    )
-    below = jnp.concatenate([masked[..., 1:, :, :], jnp.zeros_like(masked[..., :1, :, :])], axis=-3)
-    flux_down = VERT_DIFF * (below - masked) * below_open
-    flux_up = jnp.concatenate(
-        [jnp.zeros_like(flux_down[..., :1, :, :]), flux_down[..., :-1, :, :]], axis=-3
-    )
-    return flux_south - flux_north + (flux_down - flux_up)
+    surface_ref[...] = sum(weights[k] * basis[k] for k in range(SOLVER_ITERS))
+    lane = lax.broadcasted_iota(jnp.int32, (1, LANES), 1)
+    which = (lane // rows) % SOLVER_ITERS
+    scale = jnp.zeros((1, LANES), jnp.float32)
+    for k in range(SOLVER_ITERS):
+        scale = jnp.where(which == k, weights[k], scale)
+    slot = jnp.broadcast_to(lane // rows, (RING, LANES))
+    per_group = LANES // rows
+    for group in range(count // per_group):
+        joined = jnp.zeros((RING, LANES), jnp.float32)
+        for q in range(per_group):
+            scaled = moved[group * per_group + q] * scale
+            scaled = scaled + pltpu.roll(scaled, 2 * rows, 1)
+            scaled = scaled + pltpu.roll(scaled, rows, 1)
+            joined = jnp.where(slot == q, scaled, joined)
+        strip_ref[:, group * LANES : (group + 1) * LANES] = joined
+
+
+def combine_kernel(moved_ref, basis_ref, surface_ref, strip_ref):
+    combine(moved_ref, basis_ref, surface_ref, strip_ref)
 
 
 def redox_sources(masked):
@@ -196,7 +190,7 @@
     first_nitr = RATE_AMMONIUM * ammonium * with_oxygen
     second_nitr = RATE_NITRITE * nitrite * with_oxygen
     sulfide_ox = RATE_SULFIDE * sulfide * with_oxygen
-    return jnp.stack(
+    return (
         [
             -1.3 * breakdown * with_oxygen
             - 1.5 * first_nitr
@@ -216,6 +210,114 @@
     )
 
 
+def transport_kernel(
+    strip_ref, depth_ref, east_depth_ref, u_ref, v_ref, edge_ref, tracers_ref, out_ref
+):
+    z = pl.program_id(0)
+    levels = pl.num_programs(0)
+    latitudes = depth_ref.shape[1]
+    shape = depth_ref.shape
+
+    def ring(block, shift):
+        return pltpu.roll(block, shift % RING, 0)
+
+    def along(block, shift):
+        return pltpu.roll(block, shift % latitudes, 1)
+
+    column = lax.broadcasted_iota(jnp.int32, shape, 1)
+    depth = depth_ref[...]
+    is_wet = depth > z
+    wet = is_wet.astype(jnp.float32)
+    below = depth > z + 1
+    above = jnp.logical_and(is_wet, z > 0)
+    strip = strip_ref[...]
+    own = strip[: shape[0]]
+    flow_edge = edge_ref[TRACERS, 0]
+    east_depth = jnp.concatenate(
+        [east_depth_ref[...].astype(jnp.float32), ring_edge(flow_edge)], axis=0
+    )
+    east_open = (east_depth > z.astype(jnp.float32)).astype(jnp.float32)
+    u_ext = jnp.concatenate([u_ref[0], flow_edge], axis=0)
+    east_flow = (u_ext - BARO_GAIN * (ring(strip, -1) - strip)) * east_open * (1.0 / 12.0)
+    east_mix = HORIZ_DIFF * east_open
+    last = column == latitudes - 1
+    north_open = jnp.where(last, 0.0, wet * along(wet, -1))
+    north_flow = (v_ref[0] - BARO_GAIN * (along(own, -1) - own)) * north_open * (1.0 / 12.0)
+    north_mix = HORIZ_DIFF * north_open
+    first = column == 0
+    z_down = jnp.minimum(z + 1, levels - 1)
+    z_up = jnp.maximum(z - 1, 0)
+
+    masked_all = []
+    transport = []
+    for k in range(TRACERS):
+        raw = tracers_ref[k, z]
+        masked = raw * wet
+        masked_all.append(masked)
+        extended = jnp.concatenate([masked, edge_ref[k, 0]], axis=0)
+        east_one = ring(extended, -1)
+        pair = extended + east_one
+        face = 8.0 * pair - (ring(pair, 1) + ring(pair, -1))
+        flux = east_flow * face - east_mix * (east_one - extended)
+        change = (ring(flux, 1) - flux)[: shape[0]]
+        north_one = jnp.where(last, 0.0, along(masked, -1))
+        pair = masked + north_one
+        south_pair = jnp.where(first, masked, along(pair, 1))
+        north_pair = jnp.where(last, 0.0, along(pair, -1))
+        face = 8.0 * pair - (south_pair + north_pair)
+        flux = north_flow * face - north_mix * (north_one - masked)
+        change = change + (along(flux, 1) - flux)
+        down = jnp.where(below, tracers_ref[k, z_down] - raw, 0.0)
+        up = jnp.where(above, raw - tracers_ref[k, z_up], 0.0)
+        out_ref[k, 0] = raw + wet * (change + VERT_DIFF * (down - up))
+    sources = redox_sources(masked_all)
+    for k in range(TRACERS):
+        out_ref[k, 0] += wet * sources[k]
+
+
+def ring_edge(flow_edge):
+    return pltpu.roll(flow_edge, 1, 0)
+
+
+def transport(strip, column_depth, east_depth, u_clinic, v_clinic, edges, tracers):
+    count, levels, width, latitudes = tracers.shape
+    whole = lambda shape: pl.BlockSpec(shape, lambda z: (0,) * len(shape))
+    level = lambda rows: pl.BlockSpec((1, rows, latitudes), lambda z: (z, 0, 0))
+    return pl.pallas_call(
+        transport_kernel,
+        grid=(levels,),
+        in_specs=[
+            whole(strip.shape),
+            whole(column_depth.shape),
+            whole(east_depth.shape),
+            level(width),
+            level(width),
+            pl.BlockSpec((count + 1, 1, RING - width, latitudes), lambda z: (0, z, 0, 0)),
+            whole(tracers.shape),
+        ],
+        out_specs=pl.BlockSpec((count, 1, width, latitudes), lambda z: (0, z, 0, 0)),
+        out_shape=jax.ShapeDtypeStruct(tracers.shape, jnp.float32),
+        compiler_params=pltpu.CompilerParams(vmem_limit_bytes=40 * 2**20),
+    )(strip, column_depth, east_depth, u_clinic, v_clinic, edges, tracers)
+
+
+def edge_blocks(column_depth, east_depth, u_clinic, tracers):
+    levels = tracers.shape[1]
+    index = lax.broadcasted_iota(jnp.int32, (levels, 1, 1), 0)
+
+    def masked(where):
+        wet = index < column_depth[None, where]
+        return jnp.where(wet[None], tracers[:, :, where], 0.0)
+
+    ends = jnp.broadcast_to(east_depth[None, -1:].astype(jnp.float32), u_clinic[:, -1:].shape)
+    flow = jnp.concatenate([ends, u_clinic[:, -1:]], axis=1)
+    low = jnp.concatenate([masked(slice(-2, None)), flow[None]], axis=0)
+    low = shifted(low, "lon", 1, True)
+    high = shifted(masked(slice(0, 2)), "lon", -1, True)
+    high = jnp.pad(high, ((0, 1), (0, 0), (0, RING - WIDTH - 4), (0, 0)))
+    return jnp.concatenate([high, low], axis=2)
+
+
 def body(
     surface_old,
     surface_forcing,
@@ -227,38 +329,13 @@
     u_clinic,
     v_clinic,
 ):
-    surface, wide_strip = solve_and_hand_over(
+    surface, strip = solve_and_hand_over(
         surface_old, surface_forcing, surface_coeff, ocean_mask
     )
-    strip_surface = wide_strip[1:-1]
-    wide_baro = -BARO_GAIN * (wide_strip[1:] - wide_strip[:-1])
-    east_baro = wide_baro[1:]
-    above_surface = jnp.concatenate([strip_surface[:, 1:], strip_surface[:, -1:]], axis=1)
-    north_baro = -BARO_GAIN * (above_surface - strip_surface)
-    wet, east_open, north_open, below_open, east_flow, north_flow = open_faces(
-        column_depth, east_depth, east_baro, north_baro, u_clinic, v_clinic
-    )
-    masked = tracers * wet[None]
-    columns_here = masked.shape[2]
-    low, high = padded_2(masked, 2)
-    tracer_pad = jnp.concatenate([low, masked, high], axis=2)
-    west_u = shifted(u_clinic[:, -1:], "lon", 1, True)
-    west_open = shifted(east_open[:, -1:], "lon", 1, True)
-    west_flow = (west_u + wide_baro[None, :1]) * west_open
-    flow_all = jnp.concatenate([west_flow, east_flow], axis=1)
-    open_all = jnp.concatenate([west_open, east_open], axis=1)
-    center = tracer_pad[:, :, 1 : columns_here + 2]
-    east_one = tracer_pad[:, :, 2 : columns_here + 3]
-    west_one = tracer_pad[:, :, 0 : columns_here + 1]
-    east_two = tracer_pad[:, :, 3 : columns_here + 4]
-    face_east = (7.0 * (center + east_one) - (west_one + east_two)) / 12.0
-    flux_all = flow_all[None] * face_east - HORIZ_DIFF * (east_one - center) * open_all[None]
-    conv_east = flux_all[:, :, :-1] - flux_all[:, :, 1:]
-    transport = conv_east + meridional_vertical(
-        masked, north_flow[None], north_open[None], below_open[None]
-    )
-    tendency = transport + redox_sources(masked)
-    tracers_new = tracers + wet[None] * tendency
+    edges = edge_blocks(column_depth, east_depth, u_clinic, tracers)
+    tracers_new = transport(
+        strip, column_depth, east_depth, u_clinic, v_clinic, edges, tracers
+    )
     return (surface, tracers_new)
 
 

time: 135 us -> 68.6 us (0.51)
  between operations: 39.5 us -> 0.95 us
  other arithmetic: 46.6 us -> 9.7 us
  Pallas kernels: 0 us -> 18.9 us
  local copies, waits for them, and re-layouts: 31.1 us -> 14.8 us
  waiting for transfers between devices: 0.28 us -> 8.36 us
    pallas_call x0 -> x2, Pallas kernels: none -> 18.9 us  [the longest x1 15.9 us: transport(): pl.pallas_call(transport_kernel, grid=(levels,), in_specs=[whole(strip.sh...]
    add x2 -> x0, other arithmetic: 13 us -> none  [the longest x1 11.9 us: body(): tracers_new = tracers + wet[None] * tendency]
    mul x8 -> x0, other arithmetic: 9.87 us -> none  [the longest x1 4.73 us: body(): masked = tracers * wet[None]]
    sub x2 -> x0, other arithmetic: 8.96 us -> none  [the longest x1 5.36 us: meridional_vertical(): north_flow * face_north - HORIZ_DIFF * (north_one - masked) * north_open]
    slice x19 -> x7, local copies, waits for them, and re-layouts: 9.41 us -> 1.09 us  [the longest x1 0.74 us: masked(): wet = index < column_depth[None, where]]
    all_to_all x1, waiting for transfers between devices: 0.26 us -> 8.35 us  [solve_and_hand_over(): lax.all_to_all(payload, 'lon', split_axis=0, concat_axis=0, tiled=True)]
    unnamed x23 -> x16, local copies, waits for them, and re-layouts: 10.8 us -> 3.15 us
    unnamed x7 -> x0, other arithmetic: 7.27 us -> none
  transfers between devices with their start and end apart: 7 -> 5, of which waited for: 1 -> 1; matrix products, arithmetic and copies ran while one was open for 39% -> 27% of each run, Pallas kernels for 0% -> 4%
where the time goes in v2:
time: 68.6 us; the launch traced here: 67.9 us
  Pallas kernels  18.9 us (28%)
  starting transfers between devices  15.1 us (22%)
  local copies, waits for them, and re-layouts  14.8 us (22%)
  other arithmetic  9.7 us (14%)
  waiting for transfers between devices  8.36 us (12%)
  between operations  0.95 us (1%)
    pallas_call x1, Pallas kernels, transport(): pl.pallas_call(transport_kernel, grid=(levels,), in_specs=[whole(strip.sh...  15.9 us
    ppermute x4, starting transfers between devices, shifted(): return lax.ppermute(block, axis_name, pairs)  9.36 us
    another operation x1, local copies, waits for them, and re-layouts, solve_and_hand_over(): partial = jnp.stack([jnp.sum(basis[i] * basis[j]) for i, j in GRAM_PAIRS])  8.83 us
    all_to_all x1, waiting for transfers between devices, solve_and_hand_over(): lax.all_to_all(payload, 'lon', split_axis=0, concat_axis=0, tiled=True)  8.35 us
    all_to_all x1, starting transfers between devices, solve_and_hand_over(): lax.all_to_all(payload, 'lon', split_axis=0, concat_axis=0, tiled=True)  5.78 us
    select_n x1, other arithmetic, masked(): return jnp.where(wet[None], tracers[:, :, where], 0.0)  3.65 us
    unnamed x16, local copies, waits for them, and re-layouts  3.15 us
    pallas_call x1, Pallas kernels, solve_and_hand_over(): pl.pallas_call(combine_kernel, out_shape=(jax.ShapeDtypeStruct((rows, col...  2.98 us
  transfers between devices with their start and end apart: 5, of which 1 were waited for; matrix products, arithmetic and copies ran while one was open for 27% of the time, Pallas kernels for 4%

profile of v2, /device:TPU:0, one launch (start us, length us, event | category | flops | bytes accessed | tf_op | source)
XLA Modules:
  0.0 67.9 jit_solution(11542706589793649871)
XLA Ops:
  0.6 0.0 copy-start.7
  0.7 0.8 %convert_bitcast_fusion = f32[1,32,256]{2,1,0:T(8,128)S(1)} fusion(s32[32,256]{1,0:T(8,128)} %param.12), kind=kLoop, calls=%fused_computation.77 | loop fusion | flops 8192 | bytes 65536 | tf_op jit(solution)/shard_map/stack | solution.py:124
  1.5 0.8 %multiply_add_fusion = f32[32,256]{1,0:T(8,128)S(1)} fusion(f32[32,256]{1,0:T(8,128)} %param.10, f32[32,256]{1,0:T(8,128)} %param.11, f32[32,256]{1,0:T(8,128)} %param.9), kind=kLoop, calls=%fused_computation.78 | loop fusion | flops 16384 | bytes 131072 | tf_op jit(solution)/shard_map/add | solution.py:122
  2.3 0.7 %pad_maximum_fusion.16 = (f32[3,4,256]{2,1,0:T(4,128)S(1)}, f32[3,4,256]{2,1,0:T(4,128)S(1)}) fusion(f32[1,32,256]{2,1,0:T(8,128)S(1)} %convert_bitcast_fusion, f32[1,32,256]{2,1,0:T(8,128)} %bitcast.77, f32[1,32,256]{2,1,0:T(8,128)S(1)} %bitcast.70), kind=kLoop, calls=%fused_computation.81 | loop fusion | flops 12288 | bytes 122880 | tf_op jit(solution)/shard_map/stack | solution.py:124
  3.0 1.3 %collective-permute-start.1 = (f32[3,4,256]{2,1,0:T(4,128)S(1)}, f32[3,4,256]{2,1,0:T(4,128)S(1)}, u32[]{:S(2)}, u32[]{:S(2)}) collective-permute-start(f32[3,4,256]{2,1,0:T(4,128)S(1)} %get-tuple-element.29), channel_id=1, source_target_pairs={{1,0},{2,1},{3,2},{4,3},{5,4},{6,5},{7,6},{8,7},{9,8},{10,9},{11,1... | collective-permute-start | bytes 36872 | tf_op jit(solution)/shard_map/ppermute | solution.py:38
  4.3 3.0 %collective-permute-start = (f32[3,4,256]{2,1,0:T(4,128)S(1)}, f32[3,4,256]{2,1,0:T(4,128)S(1)}, u32[]{:S(2)}, u32[]{:S(2)}) collective-permute-start(f32[3,4,256]{2,1,0:T(4,128)S(1)} %get-tuple-element.30), channel_id=1, source_target_pairs={{0,1},{1,2},{2,3},{3,4},{4,5},{5,6},{6,7},{7,8},{8,9},{9,10},{10,1... | collective-permute-start | bytes 36872 | tf_op jit(solution)/shard_map/ppermute | solution.py:38
  7.3 0.7 %fusion.49 = (s32[2,512]{1,0:T(2,128)S(1)}, s32[2,512]{1,0:T(2,128)S(1)}) fusion(s32[16,512]{1,0:T(8,128)} %depth_ref.1), kind=kLoop, calls=%fused_computation.103 | loop fusion | bytes 16384 | tf_op jit(solution)/shard_map/slice | solution.py:309
  8.1 0.1 iota_compare_fusion.1
  8.1 3.7 %slice_select_fusion = (f32[8,16,2,512]{3,2,1,0:T(2,128)S(1)}, f32[8,16,2,512]{3,2,1,0:T(2,128)}) fusion(f32[8,16,16,512]{3,2,1,0:T(8,128)} %tracers_ref.1, pred[16,2,512]{2,1,0:T(4,128)(4,1)S(1)} %get-tuple-element.63, pred[16,2,512]{2,1,0:T(4,128)(4,1)S(1)} %get-tuple-element.64), kind=kLoop, calls=%fused_computation.20 | loop fusion | flops 262144 | bytes 2129920 | tf_op jit(solution)/shard_map/jit(_where)/select_n | solution.py:310
  11.8 5.0 %collective-permute-start.2 = (f32[8,16,2,512]{3,2,1,0:T(2,128)}, f32[8,16,2,512]{3,2,1,0:T(2,128)S(1)}, u32[]{:S(2)}, u32[]{:S(2)}) collective-permute-start(f32[8,16,2,512]{3,2,1,0:T(2,128)} %get-tuple-element.28), channel_id=1, source_target_pairs={{0,15},{1,0},{2,1},{3,2},{4,3},{5,4},{6,5},{7,6},{8,7},{9,8},{10,9... | collective-permute-start | bytes 1572872 | tf_op jit(solution)/shard_map/ppermute | solution.py:38
  16.9 0.1 maximum_bitcast_fusion
  17.0 0.3 pad_maximum_fusion.12
  17.3 0.1 collective-permute-start.3
  17.3 0.2 rev.3
  17.6 0.1 copy.12
  17.7 0.1 pad.30.clone
  17.8 0.1 fusion.48
  17.9 0.1 fusion.47
  18.0 0.1 broadcast_multiply_fusion
  18.1 0.1 fusion.45
  18.2 0.1 fusion.44
  18.3 0.1 fusion.32
  18.4 0.1 fusion.42
  18.5 0.1 fusion.41
  18.5 0.1 fusion.31
  18.7 0.1 fusion.39
  18.7 0.1 fusion.38
  18.8 0.1 maximum_add_fusion.3
  18.9 0.8 %multiply_reduce_fusion = (f32[]{:T(128)}, f32[]{:T(128)}, f32[]{:T(128)}, f32[]{:T(128)}, f32[]{:T(128)}, /*index=5*/f32[]{:T(128)}, f32[]{:T(128)}, f32[]{:T(1...) fusion(f32[40,256]{1,0:T(8,128)S(1)} %get-tuple-element.21, ...), kind=kLoop, calls=%fused_computation.63 | loop fusion | flops 303090 | bytes 467000 | tf_op jit(solution)/shard_map/reduce_sum | solution.py:127
  19.7 0.1 copy.14
  19.8 0.1 copy.15
  19.9 0.1 copy.13
  20.0 0.1 fusion.2
  20.2 0.4 copy.19
  20.5 0.3 reshape.37
  20.9 8.8 %stack.103 = f32[14]{0:T(128)S(1)} concatenate(f32[1]{0:T(128)} %bitcast.11, f32[1]{0:T(128)} %bitcast.12, f32[1]{0:T(128)} %bitcast.13, f32[1]{0:T(128)} %bitcast.14, f32[1]{0:T(128)} %bitcast.15, f32[1]{0:T(128)} %bitcast.16, f32[1]{0:T(128)} %bitcast.17, f32[1]{0:T(128)} %bitcast.18, f32[1]{0:T(128)} %bitcast.19, f32[1]{0:T(128)} %bitcast.20, f32[1]{0:T(128)} %bitcast.21, ...), dimensions={0} | concatenate | bytes 112 | tf_op jit(solution)/shard_map/stack | solution.py:127
  29.8 0.0 copy-start.2
  29.8 0.0 copy-start.3
  29.8 0.8 %pad_maximum_fusion.13 = f32[16,24,128]{2,1,0:T(8,128)} fusion(f32[16,1,128]{2,1,0:T(1,128)S(1)} %slice.237, f32[16,1,128]{2,1,0:T(1,128)S(1)} %broadcast_in_dim.40, f32[16,17,128]{2,1,0:T(8,128)S(1)} %slice.223, f32[24]{0:T(128)S(1)} %pad.30.clone), kind=kLoop, calls=%fused_computation.22 | loop fusion | flops 147456 | bytes 352352 | tf_op jit(solution)/shard_map/concatenate | solution.py:139
  30.5 5.8 %all-to-all-start = ((f32[16,24,128]{2,1,0:T(8,128)}), f32[16,24,128]{2,1,0:T(8,128)S(1)}, u32[]{:S(2)}, u32[]{:S(2)}) async-start(f32[16,24,128]{2,1,0:T(8,128)} %pad_maximum_fusion.13), calls=%async_computation | async-start | bytes 393216 | tf_op jit(solution)/shard_map/all_to_all | solution.py:140
  36.3 0.6 pad_maximum_fusion.14.basis_ref
  37.0 8.3 %all-to-all-done.moved_ref = f32[16,24,128]{2,1,0:T(8,128)S(1)} async-done(((f32[16,24,128]{2,1,0:T(8,128)}), f32[16,24,128]{2,1,0:T(8,128)S(1)}, u32[]{:S(2)}, u32[]{:S(2)}) %all-to-all-start) | async-done | bytes 196640 | tf_op jit(solution)/shard_map/all_to_all | solution.py:140
  45.3 0.7 copy-done.6
  46.0 3.0 %shard_map.104 = (f32[32,256]{1,0:T(8,128)}, f32[24,512]{1,0:T(8,128)}) custom-call(f32[16,24,128]{2,1,0:T(8,128)} %copy-done.6, f32[4,32,256]{2,1,0:T(8,128)} %pad_maximum_fusion.14.basis_ref), custom_call_target="tpu_custom_call" | custom-call | tf_op jit(solution)/shard_map/pallas_call | solution.py:141
  49.0 0.5 select_maximum_fusion.edge_ref
  49.5 0.3 copy-done.4
  49.8 2.2 %copy-done = f32[8,16,16,512]{3,2,1,0:T(8,128)S(1)} copy-done((f32[8,16,16,512]{3,2,1,0:T(8,128)S(1)}, f32[8,16,16,512]{3,2,1,0:T(8,128)}, u32[]{:S(2)}) %copy-start) | copy-done | bytes 4194328
  52.0 15.9 %shard_map.105 = f32[8,16,16,512]{3,2,1,0:T(8,128)} custom-call(f32[24,512]{1,0:T(8,128)S(1)} %copy-done.4, s32[16,512]{1,0:T(8,128)S(1)} %copy-done.3, s32[16,512]{1,0:T(8,128)S(1)} %copy-done.5, f32[16,16,512]{2,1,0:T(8,128)S(1)} %copy-done.1, f32[16,16,512]{2,1,0:T(8,128)S(1)} %copy-done.2, f32[9,16,8,512]{3,2,1,0:T(8,128)S(1)} %select_maximum_fusion.edge_ref, ...), custom_call_target="tpu_custom_call" | custom-call | tf_op jit(solution)/shard_map/pallas_call | solution.py:286
  (31 shorter events, 0.2 us)
Async XLA Ops:
  0.6 17.1 %copy-start.7 = (f32[32,256]{1,0:T(8,128)S(1)}, f32[32,256]{1,0:T(8,128)}, u32[]{:S(2)}) copy-start(f32[32,256]{1,0:T(8,128)} %param.11) | copy-start | bytes 98308
  0.6 16.2 %copy-start.5 = (s32[16,512]{1,0:T(8,128)S(1)}, s32[16,512]{1,0:T(8,128)}, u32[]{:S(2)}) copy-start(s32[16,512]{1,0:T(8,128)} %east_depth_ref.1) | copy-start | bytes 98308
  0.7 16.2 %copy-start.1 = (f32[16,16,512]{2,1,0:T(8,128)S(1)}, f32[16,16,512]{2,1,0:T(8,128)}, u32[]{:S(2)}) copy-start(f32[16,16,512]{2,1,0:T(8,128)} %u_ref.1) | copy-start | bytes 1572868
  3.0 14.7 %collective-permute-start.1 = (f32[3,4,256]{2,1,0:T(4,128)S(1)}, f32[3,4,256]{2,1,0:T(4,128)S(1)}, u32[]{:S(2)}, u32[]{:S(2)}) collective-permute-start(f32[3,4,256]{2,1,0:T(4,128)S(1)} %get-tuple-element.29), channel_id=1, source_target_pairs={{1,0},{2,1},{3,2},{4,3},{5,4},{6,5},{7,6},{8,7},{9,8},{10,9},{11,1... | collective-permute-start | bytes 36872 | tf_op jit(solution)/shard_map/ppermute | solution.py:38
  4.3 13.5 %collective-permute-start = (f32[3,4,256]{2,1,0:T(4,128)S(1)}, f32[3,4,256]{2,1,0:T(4,128)S(1)}, u32[]{:S(2)}, u32[]{:S(2)}) collective-permute-start(f32[3,4,256]{2,1,0:T(4,128)S(1)} %get-tuple-element.30), channel_id=1, source_target_pairs={{0,1},{1,2},{2,3},{3,4},{4,5},{5,6},{6,7},{7,8},{8,9},{9,10},{10,1... | collective-permute-start | bytes 36872 | tf_op jit(solution)/shard_map/ppermute | solution.py:38
  11.8 37.2 %collective-permute-start.2 = (f32[8,16,2,512]{3,2,1,0:T(2,128)}, f32[8,16,2,512]{3,2,1,0:T(2,128)S(1)}, u32[]{:S(2)}, u32[]{:S(2)}) collective-permute-start(f32[8,16,2,512]{3,2,1,0:T(2,128)} %get-tuple-element.28), channel_id=1, source_target_pairs={{0,15},{1,0},{2,1},{3,2},{4,3},{5,4},{6,5},{7,6},{8,7},{9,8},{10,9... | collective-permute-start | bytes 1572872 | tf_op jit(solution)/shard_map/ppermute | solution.py:38
  17.3 31.7 %collective-permute-start.3 = (f32[9,16,2,512]{3,2,1,0:T(2,128)S(1)}, f32[9,16,2,512]{3,2,1,0:T(2,128)S(1)}, u32[]{:S(2)}, u32[]{:S(2)}) collective-permute-start(f32[9,16,2,512]{3,2,1,0:T(2,128)S(1)} %pad_maximum_fusion.12), channel_id=1, source_target_pairs={{0,1},{1,2},{2,3},{3,4},{4,5},{5,6},{6,7},{7,8},{8,9},{9,10},{10,1... | collective-permute-start | bytes 1769480 | tf_op jit(solution)/shard_map/ppermute | solution.py:38
  29.8 19.7 %copy-start.2 = (f32[16,16,512]{2,1,0:T(8,128)S(1)}, f32[16,16,512]{2,1,0:T(8,128)}, u32[]{:S(2)}) copy-start(f32[16,16,512]{2,1,0:T(8,128)} %v_ref.1) | copy-start | bytes 1572868
  29.8 19.7 %copy-start.3 = (s32[16,512]{1,0:T(8,128)S(1)}, s32[16,512]{1,0:T(8,128)}, u32[]{:S(2)}) copy-start(s32[16,512]{1,0:T(8,128)} %depth_ref.1) | copy-start | bytes 98308
  30.5 14.8 %all-to-all-start = ((f32[16,24,128]{2,1,0:T(8,128)}), f32[16,24,128]{2,1,0:T(8,128)S(1)}, u32[]{:S(2)}, u32[]{:S(2)}) async-start(f32[16,24,128]{2,1,0:T(8,128)} %pad_maximum_fusion.13), calls=%async_computation | async-start | bytes 393216 | tf_op jit(solution)/shard_map/all_to_all | solution.py:140
  45.3 0.7 copy-start.6
  49.0 0.8 %copy-start.4 = (f32[24,512]{1,0:T(8,128)S(1)}, f32[24,512]{1,0:T(8,128)}, u32[]{:S(2)}) copy-start(f32[24,512]{1,0:T(8,128)} %get-tuple-element.5.strip_ref) | copy-start | bytes 147460
  49.8 2.2 %copy-start = (f32[8,16,16,512]{3,2,1,0:T(8,128)S(1)}, f32[8,16,16,512]{3,2,1,0:T(8,128)}, u32[]{:S(2)}) copy-start(f32[8,16,16,512]{3,2,1,0:T(8,128)} %tracers_ref.1) | copy-start | bytes 12582916

commit v3 on v2

--- a/solution.py
+++ b/solution.py
@@ -23,7 +23,7 @@
 YIELD_NITROUS = 0.3
 
 
-HALO = SOLVER_ITERS
+HALO = 8
 CENTER = 4.55
 HALF_WIDTH = 4.45
 LANES = 128
@@ -32,40 +32,37 @@
 SUM_ROW = WIDTH + 1
 
 
-def shifted(block, axis_name, step, periodic):
-    count = lax.axis_size(axis_name)
-    pairs = [(i, (i + step) % count) for i in range(count) if periodic or 0 <= i + step < count]
-    return lax.ppermute(block, axis_name, pairs)
-
-
-def extended_band(fields):
-    below = shifted(fields[:, -HALO:], "lon", 1, False)
-    above = shifted(fields[:, :HALO], "lon", -1, False)
-    top_device = lax.axis_index("lon") == lax.axis_size("lon") - 1
-    above = jnp.where(top_device, fields[:, -HALO:][:, ::-1, ::-1], above)
-    return jnp.concatenate([below, fields, above], axis=1)
-
-
-def apply_extended(values_in, mask_float, coeff):
+def apply_extended(values_in, mask_float, diagonal):
     masked = mask_float * values_in
-    edge = jnp.zeros_like(masked[:1])
-    northern = jnp.concatenate([masked[1:], edge], axis=0)
-    southern = jnp.concatenate([edge, masked[:-1]], axis=0)
-    eastern = jnp.roll(masked, -1, axis=1)
-    western = jnp.roll(masked, 1, axis=1)
-    return (coeff + 4.0 * mask_float) * values_in - mask_float * (
-        northern + southern + eastern + western
-    )
-
-
-def krylov_basis(extended):
-    right_side, coeff, mask_float = extended[0], extended[1], extended[2]
+    total, columns = masked.shape
+    northern = pltpu.roll(masked, total - 1, 0)
+    southern = pltpu.roll(masked, 1, 0)
+    eastern = pltpu.roll(masked, columns - 1, 1)
+    western = pltpu.roll(masked, 1, 1)
+    return diagonal * values_in - mask_float * (northern + southern + eastern + western)
+
+
+def krylov_basis(right_side, coeff, mask_float):
+    diagonal = (coeff + 4.0 * mask_float) - CENTER
     basis = [right_side]
     for order in range(SOLVER_ITERS):
         now = basis[-1]
-        image = (apply_extended(now, mask_float, coeff) - CENTER * now) * (1.0 / HALF_WIDTH)
+        image = apply_extended(now, mask_float, diagonal) * (1.0 / HALF_WIDTH)
         basis.append(image if order == 0 else 2.0 * image - basis[-2])
     return [field[HALO:-HALO] for field in basis]
+
+
+def reversed_both(block):
+    for axis in range(2):
+        size = block.shape[axis]
+        index = lax.broadcasted_iota(jnp.int32, block.shape, axis)
+        bit = 1
+        while bit < size:
+            up = pltpu.roll(block, size - bit, axis)
+            down = pltpu.roll(block, bit, axis)
+            block = jnp.where((index // bit) % 2 == 0, up, down)
+            bit *= 2
+    return block
 
 
 GRAM_PAIRS = [(i, j) for i in range(SOLVER_ITERS) for j in range(i, SOLVER_ITERS + 1)]
@@ -115,41 +112,148 @@
     return solution
 
 
-def solve_and_hand_over(surface_old, surface_forcing, surface_coeff, ocean_mask):
+def solve_kernel(
+    old_ref, forcing_ref, coeff_ref, mask_ref, low_ref, high_ref,
+    surface_ref, strip_ref, low_out, high_out,
+    fields, below_in, above_in, send, recv, basis_kept,
+    edge_sems, band_sems, send_sems, recv_sems,
+):
+    count = lax.axis_size("lon")
+    me = lax.axis_index("lon")
+    right, left = lax.rem(me + 1, count), lax.rem(me + count - 1, count)
+    rows, columns = old_ref.shape
+    mesh_id = pl.DeviceIdType.MESH
+
+    barrier = pltpu.get_barrier_semaphore()
+
+    def greet(step, carry):
+        other = lax.rem(me + step, count)
+        pl.semaphore_signal(barrier, inc=1, device_id={"lon": other}, device_id_type=mesh_id)
+        return carry
+
+    lax.fori_loop(1, count, greet, 0)
+    fields[0] = coeff_ref[...] * old_ref[...] + forcing_ref[...]
+    fields[1] = coeff_ref[...]
+    fields[2] = mask_ref[...].astype(jnp.float32)
+    pl.semaphore_wait(barrier, count - 1)
+
+    def remote(source, target, sems, n, device):
+        return pltpu.make_async_remote_copy(
+            src_ref=source,
+            dst_ref=target,
+            send_sem=sems.at[n, 0],
+            recv_sem=sems.at[n, 1],
+            device_id={"lon": device},
+            device_id_type=mesh_id,
+        )
+
+    copies = [
+        remote(fields.at[:, rows - HALO :], below_in, band_sems, 0, right),
+        remote(fields.at[:, :HALO], above_in, band_sems, 1, left),
+        remote(low_ref, low_out, edge_sems, 0, right),
+        remote(high_ref, high_out, edge_sems, 1, left),
+    ]
+    for copy in copies:
+        copy.start()
+    mirrored = [reversed_both(fields[n, rows - HALO :]) for n in range(3)]
+    copies[0].wait()
+    copies[1].wait()
+    bottom = me == 0
+    top = me == count - 1
+    extended = [
+        jnp.concatenate(
+            [
+                jnp.where(bottom, 0.0, below_in[n]),
+                fields[n],
+                jnp.where(top, mirrored[n], above_in[n]),
+            ],
+            axis=0,
+        )
+        for n in range(3)
+    ]
+    basis = krylov_basis(*extended)
+    lane = lax.broadcasted_iota(jnp.int32, (1, LANES), 1)
+    sums = jnp.zeros((1, LANES), jnp.float32)
+    for n, (i, j) in enumerate(GRAM_PAIRS):
+        total = jnp.sum(jnp.sum(basis[i] * basis[j], axis=0, keepdims=True), axis=1, keepdims=True)
+        sums = jnp.where(lane == n, total, sums)
+    for k in range(SOLVER_ITERS):
+        basis_kept[k] = basis[k]
+    tall = jnp.concatenate(basis[:SOLVER_ITERS] * (LANES // (SOLVER_ITERS * rows)), axis=0)
+    turned = jnp.transpose(tall)
+    row = lax.broadcasted_iota(jnp.int32, (RING - WIDTH, LANES), 0)
+    for d in range(count):
+        send[d, :WIDTH] = turned[d * WIDTH : (d + 1) * WIDTH]
+        after = (d + 1) % count * WIDTH
+        before = (d * WIDTH - 8) % columns
+        tail = jnp.where(row == SUM_ROW - WIDTH, sums, turned[after : after + 8])
+        send[d, WIDTH:] = jnp.where(row == 7, turned[before : before + 8], tail)
+
+    def block_copy(step):
+        other = lax.rem(me + step, count)
+        return pltpu.make_async_remote_copy(
+            src_ref=send.at[other],
+            dst_ref=recv.at[me],
+            send_sem=send_sems.at[step],
+            recv_sem=recv_sems.at[step],
+            device_id={"lon": other},
+            device_id_type=mesh_id,
+        )
+
+    def start_block(step, carry):
+        block_copy(step).start()
+        return carry
+
+    def wait_block(step, carry):
+        block_copy(step).wait()
+        return carry
+
+    lax.fori_loop(1, count, start_block, 0)
+    recv[me] = send[me]
+    lax.fori_loop(1, count, wait_block, 0)
+    combine(recv, basis_kept, surface_ref, strip_ref)
+    copies[2].wait()
+    copies[3].wait()
+
+
+def solve_and_hand_over(surface_old, surface_forcing, surface_coeff, ocean_mask, low, high):
     rows, columns = surface_old.shape
     count = lax.axis_size("lon")
-    width = columns // count
-    right_side = surface_coeff * surface_old + surface_forcing
-    extended = extended_band(
-        jnp.stack([right_side, surface_coeff, ocean_mask.astype(jnp.float32)])
-    )
-    basis = krylov_basis(extended)
-    partial = jnp.stack([jnp.sum(basis[i] * basis[j]) for i, j in GRAM_PAIRS])
-    stacked = jnp.stack(basis[:SOLVER_ITERS])
-    parts = stacked.reshape(SOLVER_ITERS, rows, count, width)
-    west = jnp.roll(parts[..., -1:], 1, axis=2)
-    east = jnp.roll(parts[..., :1], -1, axis=2)
-    wide = jnp.concatenate([west, parts, east], axis=-1)
-    wide = wide.transpose(2, 3, 0, 1).reshape(count, width + 2, SOLVER_ITERS * rows)
-    wide = jnp.tile(wide, (1, 1, LANES // wide.shape[2]))
-    sums = jnp.broadcast_to(
-        jnp.pad(partial, (0, LANES - len(GRAM_PAIRS)))[None, None], (count, 1, LANES)
-    )
-    spare = jnp.zeros((count, RING - width - 3, LANES), jnp.float32)
-    payload = jnp.concatenate([wide[:, 1:], sums, spare, wide[:, :1]], axis=1)
-    moved = lax.all_to_all(payload, "lon", split_axis=0, concat_axis=0, tiled=True)
+    vmem = pl.BlockSpec(memory_space=pltpu.VMEM)
+    anywhere = pl.BlockSpec(memory_space=pl.ANY)
     return pl.pallas_call(
-        combine_kernel,
+        solve_kernel,
+        in_specs=[vmem] * 4 + [anywhere] * 2,
+        out_specs=[vmem] * 2 + [anywhere] * 2,
         out_shape=(
             jax.ShapeDtypeStruct((rows, columns), jnp.float32),
             jax.ShapeDtypeStruct((RING, rows * count), jnp.float32),
+            jax.ShapeDtypeStruct(low.shape, jnp.float32),
+            jax.ShapeDtypeStruct(high.shape, jnp.float32),
         ),
-    )(moved, stacked)
+        scratch_shapes=[
+            pltpu.VMEM((3, rows, columns), jnp.float32),
+            pltpu.VMEM((3, HALO, columns), jnp.float32),
+            pltpu.VMEM((3, HALO, columns), jnp.float32),
+            pltpu.VMEM((count, RING, LANES), jnp.float32),
+            pltpu.VMEM((count, RING, LANES), jnp.float32),
+            pltpu.VMEM((SOLVER_ITERS, rows, columns), jnp.float32),
+            pltpu.SemaphoreType.DMA((2, 2)),
+            pltpu.SemaphoreType.DMA((2, 2)),
+            pltpu.SemaphoreType.DMA((count,)),
+            pltpu.SemaphoreType.DMA((count,)),
+        ],
+        compiler_params=pltpu.CompilerParams(
+            collective_id=0, has_side_effects=True, vmem_limit_bytes=8 * 2**20
+        ),
+    )(surface_old, surface_forcing, surface_coeff, ocean_mask, low, high)
 
 
 def combine(moved, basis, surface_ref, strip_ref):
     count, rows = moved.shape[0], basis.shape[1]
-    totals = jnp.sum(moved[:, SUM_ROW : SUM_ROW + 1, :], axis=0)
+    totals = moved[0, SUM_ROW : SUM_ROW + 1, :]
+    for source in range(1, count):
+        totals = totals + moved[source, SUM_ROW : SUM_ROW + 1, :]
     gram = {pair: totals[:, n : n + 1] for n, pair in enumerate(GRAM_PAIRS)}
     weights = solver_coefficients(gram)
     surface_ref[...] = sum(weights[k] * basis[k] for k in range(SOLVER_ITERS))
@@ -168,10 +272,6 @@
             scaled = scaled + pltpu.roll(scaled, rows, 1)
             joined = jnp.where(slot == q, scaled, joined)
         strip_ref[:, group * LANES : (group + 1) * LANES] = joined
-
-
-def combine_kernel(moved_ref, basis_ref, surface_ref, strip_ref):
-    combine(moved_ref, basis_ref, surface_ref, strip_ref)
 
 
 def redox_sources(masked):
@@ -312,8 +412,10 @@
     ends = jnp.broadcast_to(east_depth[None, -1:].astype(jnp.float32), u_clinic[:, -1:].shape)
     flow = jnp.concatenate([ends, u_clinic[:, -1:]], axis=1)
     low = jnp.concatenate([masked(slice(-2, None)), flow[None]], axis=0)
-    low = shifted(low, "lon", 1, True)
-    high = shifted(masked(slice(0, 2)), "lon", -1, True)
+    return low, masked(slice(0, 2))
+
+
+def ring_of(low, high):
     high = jnp.pad(high, ((0, 1), (0, 0), (0, RING - WIDTH - 4), (0, 0)))
     return jnp.concatenate([high, low], axis=2)
 
@@ -329,10 +431,11 @@
     u_clinic,
     v_clinic,
 ):
-    surface, strip = solve_and_hand_over(
-        surface_old, surface_forcing, surface_coeff, ocean_mask
+    low, high = edge_blocks(column_depth, east_depth, u_clinic, tracers)
+    surface, strip, low, high = solve_and_hand_over(
+        surface_old, surface_forcing, surface_coeff, ocean_mask, low, high
     )
-    edges = edge_blocks(column_depth, east_depth, u_clinic, tracers)
+    edges = ring_of(low, high)
     tracers_new = transport(
         strip, column_depth, east_depth, u_clinic, v_clinic, edges, tracers
     )

time: 68.6 us -> 47.8 us (0.70)
  Pallas kernels: 18.9 us -> 39.7 us
  starting transfers between devices: 15.1 us -> 0 us
  local copies, waits for them, and re-layouts: 14.8 us -> 2.4 us
  waiting for transfers between devices: 8.36 us -> 0 us
  other arithmetic: 9.7 us -> 4.45 us
    pallas_call x1, Pallas kernels: 2.98 us -> 23.8 us  [solve_and_hand_over(): pl.pallas_call(solve_kernel, in_specs=[vmem] * 4 + [anywhere] * 2, out_sp...]
    another operation x3 -> x0, local copies, waits for them, and re-layouts: 9.53 us -> none  [the longest x1 8.83 us: solve_and_hand_over(): partial = jnp.stack([jnp.sum(basis[i] * basis[j]) for i, j in GRAM_PAIRS])]
    ppermute x4 -> x0, starting transfers between devices: 9.36 us -> none  [shifted(): return lax.ppermute(block, axis_name, pairs)]
    all_to_all x1 -> x0, waiting for transfers between devices: 8.35 us -> none  [solve_and_hand_over(): lax.all_to_all(payload, 'lon', split_axis=0, concat_axis=0, tiled=True)]
    all_to_all x1 -> x0, starting transfers between devices: 5.78 us -> none  [solve_and_hand_over(): lax.all_to_all(payload, 'lon', split_axis=0, concat_axis=0, tiled=True)]
    unnamed x16 -> x19, local copies, waits for them, and re-layouts: 3.15 us -> 0.66 us
    another operation x3 -> x0, other arithmetic: 2.19 us -> none  [the longest x2 1.54 us: solve_and_hand_over(): jnp.stack([right_side, surface_coeff, ocean_mask.astype(jnp.float32)])]
    slice x1, local copies, waits for them, and re-layouts: 0.03 us -> 0.98 us  [edge_blocks(): flow = jnp.concatenate([ends, u_clinic[:, -1:]], axis=1)]
  transfers between devices with their start and end apart: 5 -> 0, of which waited for: 1 -> 0; matrix products, arithmetic and copies ran while one was open for 27% -> 0% of each run, Pallas kernels for 4% -> 0%
where the time goes in v3:
time: 47.8 us; the launch traced here: 47.4 us
  Pallas kernels  39.7 us (83%)
  other arithmetic  4.45 us (9%)
  local copies, waits for them, and re-layouts  2.4 us (5%)
  between operations  0.83 us (2%)
    pallas_call x1, Pallas kernels, solve_and_hand_over(): pl.pallas_call(solve_kernel, in_specs=[vmem] * 4 + [anywhere] * 2, out_sp...  23.8 us
    pallas_call x1, Pallas kernels, transport(): pl.pallas_call(transport_kernel, grid=(levels,), in_specs=[whole(strip.sh...  15.9 us
    select_n x1, other arithmetic, masked(): return jnp.where(wet[None], tracers[:, :, where], 0.0)  2.78 us
    slice x1, local copies, waits for them, and re-layouts, edge_blocks(): flow = jnp.concatenate([ends, u_clinic[:, -1:]], axis=1)  0.98 us

profile of v3, /device:TPU:0, one launch (start us, length us, event | category | flops | bytes accessed | tf_op | source)
XLA Modules:
  0.0 47.4 jit_solution(614137935550588919)
XLA Ops:
  0.6 0.0 copy-start.8
  0.6 0.0 copy-start.7
  0.7 0.0 copy-start.6
  0.7 0.0 copy-start.5
  0.7 0.7 %slice_convert_fusion = f32[1,512]{1,0:T(1,128)S(1)} fusion(s32[16,512]{1,0:T(8,128)} %east_depth_ref.1), kind=kLoop, calls=%fused_computation.8 | loop fusion | flops 512 | bytes 4096 | tf_op jit(solution)/shard_map/convert_element_type | solution.py:412
  1.4 0.7 %fusion = (s32[2,512]{1,0:T(2,128)S(1)}, s32[2,512]{1,0:T(2,128)S(1)}) fusion(s32[16,512]{1,0:T(8,128)} %depth_ref.1), kind=kLoop, calls=%fused_computation.9 | loop fusion | bytes 16384 | tf_op jit(solution)/shard_map/slice | solution.py:409
  2.2 1.0 %slice.21 = f32[16,1,512]{2,1,0:T(1,128)S(1)} slice(f32[16,16,512]{2,1,0:T(8,128)} %u_ref.1), slice={[0:16], [15:16], [0:512]} | slice | bytes 65536 | tf_op jit(solution)/shard_map/slice | solution.py:413
  3.2 0.1 maximum_bitcast_fusion
  3.2 0.1 iota_compare_fusion.1
  3.3 2.8 %slice_select_fusion = (f32[8,16,2,512]{3,2,1,0:T(2,128)S(1)}, f32[8,16,2,512]{3,2,1,0:T(2,128)S(1)}) fusion(f32[8,16,16,512]{3,2,1,0:T(8,128)} %tracers_ref.1, pred[16,2,512]{2,1,0:T(4,128)(4,1)S(1)} %get-tuple-element.14, pred[16,2,512]{2,1,0:T(4,128)(4,1)S(1)} %get-tuple-element.15), kind=kLoop, calls=%fused_computation.3 | loop fusion | flops 262144 | bytes 2129920 | tf_op jit(solution)/shard_map/jit(_where)/select_n | solution.py:410
  6.1 0.0 copy-start.2
  6.1 0.0 copy-start.3
  6.1 0.0 copy-start.4
  6.1 0.3 pad_maximum_fusion.low_ref
  6.4 0.0 copy-done.8
  6.5 0.0 copy-done.7
  6.5 0.0 copy-done.6
  6.5 0.0 copy-done.5
  6.5 0.0 copy-start
  6.5 0.0 copy-start.1
  6.5 23.8 %shard_map.104 = (f32[32,256]{1,0:T(8,128)S(1)}, f32[24,512]{1,0:T(8,128)S(1)}, f32[9,16,2,512]{3,2,1,0:T(2,128)S(1)}, f32[8,16,2,512]{3,2,1,0:T(2,128)S(1)}) custom-call(f32[32,256]{1,0:T(8,128)S(1)} %copy-done.5, f32[32,256]{1,0:T(8,128)S(1)} %copy-done.6, f32[32,256]{1,0:T(8,128)S(1)} %copy-done.7, s32[32,256]{1,0:T(8,128)S(1)} %copy-done.8, ...), custom_call_target="tpu_custom_call" | custom-call | tf_op jit(solution)/shard_map/pallas_call | solution.py:224
  30.3 0.5 %select_maximum_fusion.edge_ref = f32[9,16,8,512]{3,2,1,0:T(8,128)S(1)} fusion(f32[8,16,2,512]{3,2,1,0:T(2,128)S(1)} %get-tuple-element.8, f32[9,16,2,512]{3,2,1,0:T(2,128)S(1)} %get-tuple-element.9), kind=kLoop, calls=%fused_computation | loop fusion | flops 1769472 | bytes 3473408 | tf_op jit(solution)/shard_map/concatenate | solution.py:420
  30.8 0.0 copy-done.2
  30.8 0.0 copy-done.3
  30.8 0.0 copy-done.4
  30.8 0.0 copy-done
  30.8 0.0 copy-done.1
  30.8 15.9 %shard_map.105 = f32[8,16,16,512]{3,2,1,0:T(8,128)} custom-call(f32[24,512]{1,0:T(8,128)S(1)} %get-tuple-element.7.strip_ref, s32[16,512]{1,0:T(8,128)S(1)} %copy-done.3, s32[16,512]{1,0:T(8,128)S(1)} %copy-done.4, f32[16,16,512]{2,1,0:T(8,128)S(1)} %copy-done.1, f32[16,16,512]{2,1,0:T(8,128)S(1)} %copy-done.2, ...), custom_call_target="tpu_custom_call" | custom-call | tf_op jit(solution)/shard_map/pallas_call | solution.py:386
  46.8 0.6 %copy.12 = f32[32,256]{1,0:T(8,128)} copy(f32[32,256]{1,0:T(8,128)S(1)} %get-tuple-element.18) | data formatting | bytes 65536
  (1 shorter events, 0.0 us)
Async XLA Ops:
  0.6 5.8 %copy-start.8 = (s32[32,256]{1,0:T(8,128)S(1)}, s32[32,256]{1,0:T(8,128)}, u32[]{:S(2)}) copy-start(s32[32,256]{1,0:T(8,128)} %mask_ref.1) | copy-start | bytes 98308
  0.6 5.8 %copy-start.7 = (f32[32,256]{1,0:T(8,128)S(1)}, f32[32,256]{1,0:T(8,128)}, u32[]{:S(2)}) copy-start(f32[32,256]{1,0:T(8,128)} %coeff_ref.1) | copy-start | bytes 98308
  0.7 5.8 %copy-start.6 = (f32[32,256]{1,0:T(8,128)S(1)}, f32[32,256]{1,0:T(8,128)}, u32[]{:S(2)}) copy-start(f32[32,256]{1,0:T(8,128)} %forcing_ref.1) | copy-start | bytes 98308
  0.7 5.8 %copy-start.5 = (f32[32,256]{1,0:T(8,128)S(1)}, f32[32,256]{1,0:T(8,128)}, u32[]{:S(2)}) copy-start(f32[32,256]{1,0:T(8,128)} %old_ref.1) | copy-start | bytes 98308
  6.1 24.7 %copy-start.2 = (f32[16,16,512]{2,1,0:T(8,128)S(1)}, f32[16,16,512]{2,1,0:T(8,128)}, u32[]{:S(2)}) copy-start(f32[16,16,512]{2,1,0:T(8,128)} %v_ref.1) | copy-start | bytes 1572868
  6.1 24.7 %copy-start.3 = (s32[16,512]{1,0:T(8,128)S(1)}, s32[16,512]{1,0:T(8,128)}, u32[]{:S(2)}) copy-start(s32[16,512]{1,0:T(8,128)} %depth_ref.1) | copy-start | bytes 98308
  6.1 24.7 %copy-start.4 = (s32[16,512]{1,0:T(8,128)S(1)}, s32[16,512]{1,0:T(8,128)}, u32[]{:S(2)}) copy-start(s32[16,512]{1,0:T(8,128)} %east_depth_ref.1) | copy-start | bytes 98308
  6.5 24.3 %copy-start = (f32[8,16,16,512]{3,2,1,0:T(8,128)S(1)}, f32[8,16,16,512]{3,2,1,0:T(8,128)}, u32[]{:S(2)}) copy-start(f32[8,16,16,512]{3,2,1,0:T(8,128)} %tracers_ref.1) | copy-start | bytes 12582916
  6.5 24.3 %copy-start.1 = (f32[16,16,512]{2,1,0:T(8,128)S(1)}, f32[16,16,512]{2,1,0:T(8,128)}, u32[]{:S(2)}) copy-start(f32[16,16,512]{2,1,0:T(8,128)} %u_ref.1) | copy-start | bytes 1572868

commit v4 on v3

--- a/solution.py
+++ b/solution.py
@@ -113,8 +113,8 @@
 
 
 def solve_kernel(
-    old_ref, forcing_ref, coeff_ref, mask_ref, low_ref, high_ref,
-    surface_ref, strip_ref, low_out, high_out,
+    old_ref, forcing_ref, coeff_ref, mask_ref, depth_ref, tracers_ref, low_ref, high_ref,
+    surface_ref, strip_ref, partial_ref, low_out, high_out,
     fields, below_in, above_in, send, recv, basis_kept,
     edge_sems, band_sems, send_sems, recv_sems,
 ):
@@ -210,24 +210,50 @@
 
     lax.fori_loop(1, count, start_block, 0)
     recv[me] = send[me]
+    column_terms(depth_ref, tracers_ref, partial_ref)
     lax.fori_loop(1, count, wait_block, 0)
     combine(recv, basis_kept, surface_ref, strip_ref)
     copies[2].wait()
     copies[3].wait()
 
 
-def solve_and_hand_over(surface_old, surface_forcing, surface_coeff, ocean_mask, low, high):
+def column_terms(depth_ref, tracers_ref, partial_ref):
+    levels = tracers_ref.shape[1]
+
+    def one_level(z, carry):
+        depth = depth_ref[...]
+        is_wet = depth > z
+        wet = is_wet.astype(jnp.float32)
+        below = depth > z + 1
+        above = jnp.logical_and(is_wet, z > 0)
+        z_down = jnp.minimum(z + 1, levels - 1)
+        z_up = jnp.maximum(z - 1, 0)
+        sources = redox_sources([tracers_ref[k, z] * wet for k in range(TRACERS)])
+        for k in range(TRACERS):
+            raw = tracers_ref[k, z]
+            down = jnp.where(below, tracers_ref[k, z_down] - raw, 0.0)
+            up = jnp.where(above, raw - tracers_ref[k, z_up], 0.0)
+            partial_ref[k, z] = raw + wet * (VERT_DIFF * (down - up) + sources[k])
+        return carry
+
+    lax.fori_loop(0, levels, one_level, 0)
+
+
+def solve_and_hand_over(
+    surface_old, surface_forcing, surface_coeff, ocean_mask, column_depth, tracers, low, high
+):
     rows, columns = surface_old.shape
     count = lax.axis_size("lon")
     vmem = pl.BlockSpec(memory_space=pltpu.VMEM)
     anywhere = pl.BlockSpec(memory_space=pl.ANY)
     return pl.pallas_call(
         solve_kernel,
-        in_specs=[vmem] * 4 + [anywhere] * 2,
-        out_specs=[vmem] * 2 + [anywhere] * 2,
+        in_specs=[vmem] * 6 + [anywhere] * 2,
+        out_specs=[vmem] * 3 + [anywhere] * 2,
         out_shape=(
             jax.ShapeDtypeStruct((rows, columns), jnp.float32),
             jax.ShapeDtypeStruct((RING, rows * count), jnp.float32),
+            jax.ShapeDtypeStruct(tracers.shape, jnp.float32),
             jax.ShapeDtypeStruct(low.shape, jnp.float32),
             jax.ShapeDtypeStruct(high.shape, jnp.float32),
         ),
@@ -244,9 +270,11 @@
             pltpu.SemaphoreType.DMA((count,)),
         ],
         compiler_params=pltpu.CompilerParams(
-            collective_id=0, has_side_effects=True, vmem_limit_bytes=8 * 2**20
+            collective_id=0, has_side_effects=True, vmem_limit_bytes=20 * 2**20
         ),
-    )(surface_old, surface_forcing, surface_coeff, ocean_mask, low, high)
+    )(
+        surface_old, surface_forcing, surface_coeff, ocean_mask, column_depth, tracers, low, high
+    )
 
 
 def combine(moved, basis, surface_ref, strip_ref):
@@ -311,10 +339,9 @@
 
 
 def transport_kernel(
-    strip_ref, depth_ref, east_depth_ref, u_ref, v_ref, edge_ref, tracers_ref, out_ref
+    strip_ref, depth_ref, east_depth_ref, u_ref, v_ref, edge_ref, tracers_ref, partial_ref, out_ref
 ):
     z = pl.program_id(0)
-    levels = pl.num_programs(0)
     latitudes = depth_ref.shape[1]
     shape = depth_ref.shape
 
@@ -326,10 +353,7 @@
 
     column = lax.broadcasted_iota(jnp.int32, shape, 1)
     depth = depth_ref[...]
-    is_wet = depth > z
-    wet = is_wet.astype(jnp.float32)
-    below = depth > z + 1
-    above = jnp.logical_and(is_wet, z > 0)
+    wet = (depth > z).astype(jnp.float32)
     strip = strip_ref[...]
     own = strip[: shape[0]]
     flow_edge = edge_ref[TRACERS, 0]
@@ -345,15 +369,9 @@
     north_flow = (v_ref[0] - BARO_GAIN * (along(own, -1) - own)) * north_open * (1.0 / 12.0)
     north_mix = HORIZ_DIFF * north_open
     first = column == 0
-    z_down = jnp.minimum(z + 1, levels - 1)
-    z_up = jnp.maximum(z - 1, 0)
-
-    masked_all = []
-    transport = []
+
     for k in range(TRACERS):
-        raw = tracers_ref[k, z]
-        masked = raw * wet
-        masked_all.append(masked)
+        masked = tracers_ref[k, 0] * wet
         extended = jnp.concatenate([masked, edge_ref[k, 0]], axis=0)
         east_one = ring(extended, -1)
         pair = extended + east_one
@@ -367,22 +385,18 @@
         face = 8.0 * pair - (south_pair + north_pair)
         flux = north_flow * face - north_mix * (north_one - masked)
         change = change + (along(flux, 1) - flux)
-        down = jnp.where(below, tracers_ref[k, z_down] - raw, 0.0)
-        up = jnp.where(above, raw - tracers_ref[k, z_up], 0.0)
-        out_ref[k, 0] = raw + wet * (change + VERT_DIFF * (down - up))
-    sources = redox_sources(masked_all)
-    for k in range(TRACERS):
-        out_ref[k, 0] += wet * sources[k]
+        out_ref[k, 0] = partial_ref[k, 0] + wet * change
 
 
 def ring_edge(flow_edge):
     return pltpu.roll(flow_edge, 1, 0)
 
 
-def transport(strip, column_depth, east_depth, u_clinic, v_clinic, edges, tracers):
+def transport(strip, column_depth, east_depth, u_clinic, v_clinic, edges, tracers, partial):
     count, levels, width, latitudes = tracers.shape
     whole = lambda shape: pl.BlockSpec(shape, lambda z: (0,) * len(shape))
     level = lambda rows: pl.BlockSpec((1, rows, latitudes), lambda z: (z, 0, 0))
+    cut = pl.BlockSpec((count, 1, width, latitudes), lambda z: (0, z, 0, 0))
     return pl.pallas_call(
         transport_kernel,
         grid=(levels,),
@@ -393,12 +407,13 @@
             level(width),
             level(width),
             pl.BlockSpec((count + 1, 1, RING - width, latitudes), lambda z: (0, z, 0, 0)),
-            whole(tracers.shape),
+            cut,
+            cut,
         ],
-        out_specs=pl.BlockSpec((count, 1, width, latitudes), lambda z: (0, z, 0, 0)),
+        out_specs=cut,
         out_shape=jax.ShapeDtypeStruct(tracers.shape, jnp.float32),
         compiler_params=pltpu.CompilerParams(vmem_limit_bytes=40 * 2**20),
-    )(strip, column_depth, east_depth, u_clinic, v_clinic, edges, tracers)
+    )(strip, column_depth, east_depth, u_clinic, v_clinic, edges, tracers, partial)
 
 
 def edge_blocks(column_depth, east_depth, u_clinic, tracers):
@@ -432,12 +447,12 @@
     v_clinic,
 ):
     low, high = edge_blocks(column_depth, east_depth, u_clinic, tracers)
-    surface, strip, low, high = solve_and_hand_over(
-        surface_old, surface_forcing, surface_coeff, ocean_mask, low, high
+    surface, strip, partial, low, high = solve_and_hand_over(
+        surface_old, surface_forcing, surface_coeff, ocean_mask, column_depth, tracers, low, high
     )
     edges = ring_of(low, high)
     tracers_new = transport(
-        strip, column_depth, east_depth, u_clinic, v_clinic, edges, tracers
+        strip, column_depth, east_depth, u_clinic, v_clinic, edges, tracers, partial
     )
     return (surface, tracers_new)
 

time: 47.8 us -> 48.9 us (1.023)
  local copies, waits for them, and re-layouts: 2.4 us -> 5.24 us
  Pallas kernels: 39.7 us -> 38 us
    unnamed x19 -> x21, local copies, waits for them, and re-layouts: 0.66 us -> 3.5 us
    pallas_call x1, Pallas kernels: 15.9 us -> 14.3 us  [transport(): pl.pallas_call(transport_kernel, grid=(levels,), in_specs=[whole(strip.sh...]
where the time goes in v4:
time: 48.9 us; the launch traced here: 48.5 us
  Pallas kernels  38 us (78%)
  local copies, waits for them, and re-layouts  5.24 us (11%)
  other arithmetic  4.48 us (9%)
  between operations  0.81 us (2%)
    pallas_call x1, Pallas kernels, solve_and_hand_over(): pl.pallas_call(solve_kernel, in_specs=[vmem] * 6 + [anywhere] * 2, out_sp...  23.7 us
    pallas_call x1, Pallas kernels, transport(): pl.pallas_call(transport_kernel, grid=(levels,), in_specs=[whole(strip.sh...  14.3 us
    unnamed x21, local copies, waits for them, and re-layouts  3.5 us
    select_n x1, other arithmetic, masked(): return jnp.where(wet[None], tracers[:, :, where], 0.0)  2.8 us
    slice x1, local copies, waits for them, and re-layouts, edge_blocks(): flow = jnp.concatenate([ends, u_clinic[:, -1:]], axis=1)  0.98 us

profile of v4, /device:TPU:0, one launch (start us, length us, event | category | flops | bytes accessed | tf_op | source)
XLA Modules:
  0.0 48.5 jit_solution(17694148199836597936)
XLA Ops:
  0.6 0.0 copy-start.4
  0.6 0.0 copy-start.9
  0.7 0.0 copy-start.8
  0.7 0.0 copy-start.7
  0.7 0.0 copy-start.6
  0.7 0.8 %slice_convert_fusion = f32[1,512]{1,0:T(1,128)S(1)} fusion(s32[16,512]{1,0:T(8,128)} %east_depth_ref.1), kind=kLoop, calls=%fused_computation.8 | loop fusion | flops 512 | bytes 4096 | tf_op jit(solution)/shard_map/convert_element_type | solution.py:427
  1.4 0.7 %fusion = (s32[2,512]{1,0:T(2,128)S(1)}, s32[2,512]{1,0:T(2,128)S(1)}) fusion(s32[16,512]{1,0:T(8,128)} %depth_ref.3), kind=kLoop, calls=%fused_computation.9 | loop fusion | bytes 16384 | tf_op jit(solution)/shard_map/slice | solution.py:424
  2.2 1.0 %slice.21 = f32[16,1,512]{2,1,0:T(1,128)S(1)} slice(f32[16,16,512]{2,1,0:T(8,128)} %u_ref.1), slice={[0:16], [15:16], [0:512]} | slice | bytes 65536 | tf_op jit(solution)/shard_map/slice | solution.py:428
  3.2 0.1 maximum_bitcast_fusion
  3.3 0.1 iota_compare_fusion.1
  3.3 2.8 %slice_select_fusion = (f32[8,16,2,512]{3,2,1,0:T(2,128)S(1)}, f32[8,16,2,512]{3,2,1,0:T(2,128)S(1)}) fusion(f32[8,16,16,512]{3,2,1,0:T(8,128)} %tracers_ref.3, pred[16,2,512]{2,1,0:T(4,128)(4,1)S(1)} %get-tuple-element.16, pred[16,2,512]{2,1,0:T(4,128)(4,1)S(1)} %get-tuple-element.17), kind=kLoop, calls=%fused_computation.3 | loop fusion | flops 262144 | bytes 2129920 | tf_op jit(solution)/shard_map/jit(_where)/select_n | solution.py:425
  6.1 0.3 pad_maximum_fusion.low_ref
  6.4 0.0 copy-done.4
  6.5 0.0 copy-done.9
  6.5 0.0 copy-done.8
  6.5 0.0 copy-done.7
  6.5 0.0 copy-done.6
  6.5 0.0 copy-start
  6.5 2.2 %copy-done = f32[8,16,16,512]{3,2,1,0:T(8,128)S(1)} copy-done((f32[8,16,16,512]{3,2,1,0:T(8,128)S(1)}, f32[8,16,16,512]{3,2,1,0:T(8,128)}, u32[]{:S(2)}) %copy-start) | copy-done | bytes 4194328
  8.7 0.0 copy-start.1
  8.7 23.7 %shard_map.104 = (f32[32,256]{1,0:T(8,128)S(1)}, f32[24,512]{1,0:T(8,128)S(1)}, f32[8,16,16,512]{3,2,1,0:T(8,128)S(1)}, f32[9,16,2,512]{3,2,1,0:T(2,128)S(1)}, f32[8,16,2,512]{3,2,1,0:T(2,128)S(1)}) custom-call(f32[32,256]{1,0:T(8,128)S(1)} %copy-done.6, f32[32,256]{1,0:T(8,128)S(1)} %copy-done.7, f32[32,256]{1,0:T(8,128)S(1)} %copy-done.8, ...), custom_call_target="tpu_custom_call" | custom-call | tf_op jit(solution)/shard_map/pallas_call | solution.py:249
  32.4 0.0 copy-start.2
  32.4 0.0 copy-start.3
  32.4 0.0 copy-start.5
  32.4 0.5 %select_maximum_fusion.edge_ref = f32[9,16,8,512]{3,2,1,0:T(8,128)S(1)} fusion(f32[8,16,2,512]{3,2,1,0:T(2,128)S(1)} %get-tuple-element.9, f32[9,16,2,512]{3,2,1,0:T(2,128)S(1)} %get-tuple-element.10), kind=kLoop, calls=%fused_computation | loop fusion | flops 1769472 | bytes 3473408 | tf_op jit(solution)/shard_map/concatenate | solution.py:435
  32.9 0.0 copy-done.1
  32.9 0.5 %copy-done.2 = f32[16,16,512]{2,1,0:T(8,128)S(1)} copy-done((f32[16,16,512]{2,1,0:T(8,128)S(1)}, f32[16,16,512]{2,1,0:T(8,128)}, u32[]{:S(2)}) %copy-start.2) | copy-done | bytes 524312
  33.4 0.2 copy-done.3
  33.6 0.0 copy-done.5
  33.6 14.3 %shard_map.105 = f32[8,16,16,512]{3,2,1,0:T(8,128)} custom-call(f32[24,512]{1,0:T(8,128)S(1)} %get-tuple-element.8.strip_ref, s32[16,512]{1,0:T(8,128)S(1)} %copy-done.4, s32[16,512]{1,0:T(8,128)S(1)} %copy-done.5, f32[16,16,512]{2,1,0:T(8,128)S(1)} %copy-done.2, f32[16,16,512]{2,1,0:T(8,128)S(1)} %copy-done.3, ...), custom_call_target="tpu_custom_call" | custom-call | tf_op jit(solution)/shard_map/pallas_call | solution.py:400
  47.9 0.6 %copy.12 = f32[32,256]{1,0:T(8,128)} copy(f32[32,256]{1,0:T(8,128)S(1)} %get-tuple-element.20) | data formatting | bytes 65536
  (1 shorter events, 0.0 us)
Async XLA Ops:
  0.6 5.8 %copy-start.4 = (s32[16,512]{1,0:T(8,128)S(1)}, s32[16,512]{1,0:T(8,128)}, u32[]{:S(2)}) copy-start(s32[16,512]{1,0:T(8,128)} %depth_ref.3) | copy-start | bytes 98308
  0.6 5.8 %copy-start.9 = (s32[32,256]{1,0:T(8,128)S(1)}, s32[32,256]{1,0:T(8,128)}, u32[]{:S(2)}) copy-start(s32[32,256]{1,0:T(8,128)} %mask_ref.1) | copy-start | bytes 98308
  0.7 5.8 %copy-start.8 = (f32[32,256]{1,0:T(8,128)S(1)}, f32[32,256]{1,0:T(8,128)}, u32[]{:S(2)}) copy-start(f32[32,256]{1,0:T(8,128)} %coeff_ref.1) | copy-start | bytes 98308
  0.7 5.8 %copy-start.7 = (f32[32,256]{1,0:T(8,128)S(1)}, f32[32,256]{1,0:T(8,128)}, u32[]{:S(2)}) copy-start(f32[32,256]{1,0:T(8,128)} %forcing_ref.1) | copy-start | bytes 98308
  0.7 5.8 %copy-start.6 = (f32[32,256]{1,0:T(8,128)S(1)}, f32[32,256]{1,0:T(8,128)}, u32[]{:S(2)}) copy-start(f32[32,256]{1,0:T(8,128)} %old_ref.1) | copy-start | bytes 98308
  6.5 2.2 %copy-start = (f32[8,16,16,512]{3,2,1,0:T(8,128)S(1)}, f32[8,16,16,512]{3,2,1,0:T(8,128)}, u32[]{:S(2)}) copy-start(f32[8,16,16,512]{3,2,1,0:T(8,128)} %tracers_ref.3) | copy-start | bytes 12582916
  8.7 24.2 %copy-start.1 = (f32[8,16,16,512]{3,2,1,0:T(8,128)S(1)}, f32[8,16,16,512]{3,2,1,0:T(8,128)}, u32[]{:S(2)}) copy-start(f32[8,16,16,512]{3,2,1,0:T(8,128)} %tracers_ref.3) | copy-start | bytes 12582916
  32.4 1.0 %copy-start.2 = (f32[16,16,512]{2,1,0:T(8,128)S(1)}, f32[16,16,512]{2,1,0:T(8,128)}, u32[]{:S(2)}) copy-start(f32[16,16,512]{2,1,0:T(8,128)} %u_ref.1) | copy-start | bytes 1572868
  32.4 1.2 %copy-start.3 = (f32[16,16,512]{2,1,0:T(8,128)S(1)}, f32[16,16,512]{2,1,0:T(8,128)}, u32[]{:S(2)}) copy-start(f32[16,16,512]{2,1,0:T(8,128)} %v_ref.1) | copy-start | bytes 1572868
  32.4 1.2 %copy-start.5 = (s32[16,512]{1,0:T(8,128)S(1)}, s32[16,512]{1,0:T(8,128)}, u32[]{:S(2)}) copy-start(s32[16,512]{1,0:T(8,128)} %east_depth_ref.1) | copy-start | bytes 98308

commit v5 on v4

--- a/solution.py
+++ b/solution.py
@@ -113,10 +113,10 @@
 
 
 def solve_kernel(
-    old_ref, forcing_ref, coeff_ref, mask_ref, depth_ref, tracers_ref, low_ref, high_ref,
+    old_ref, forcing_ref, coeff_ref, mask_ref, depth_ref, tracers_hbm, v_hbm, low_ref, high_ref,
     surface_ref, strip_ref, partial_ref, low_out, high_out,
-    fields, below_in, above_in, send, recv, basis_kept,
-    edge_sems, band_sems, send_sems, recv_sems,
+    fields, below_in, above_in, send, recv, basis_kept, tracers_ref, v_ref,
+    edge_sems, band_sems, send_sems, recv_sems, local_sems,
 ):
     count = lax.axis_size("lon")
     me = lax.axis_index("lon")
@@ -132,6 +132,12 @@
         return carry
 
     lax.fori_loop(1, count, greet, 0)
+    fetches = [
+        pltpu.make_async_copy(tracers_hbm, tracers_ref, local_sems.at[0]),
+        pltpu.make_async_copy(v_hbm, v_ref, local_sems.at[1]),
+    ]
+    for fetch in fetches:
+        fetch.start()
     fields[0] = coeff_ref[...] * old_ref[...] + forcing_ref[...]
     fields[1] = coeff_ref[...]
     fields[2] = mask_ref[...].astype(jnp.float32)
@@ -210,9 +216,12 @@
 
     lax.fori_loop(1, count, start_block, 0)
     recv[me] = send[me]
+    fetches[0].wait()
+    fetches[1].wait()
     column_terms(depth_ref, tracers_ref, partial_ref)
     lax.fori_loop(1, count, wait_block, 0)
     combine(recv, basis_kept, surface_ref, strip_ref)
+    north_terms(strip_ref, depth_ref, v_ref, tracers_ref, partial_ref)
     copies[2].wait()
     copies[3].wait()
 
@@ -239,8 +248,46 @@
     lax.fori_loop(0, levels, one_level, 0)
 
 
+def north_terms(strip_ref, depth_ref, v_ref, tracers_ref, partial_ref):
+    shape = depth_ref.shape
+    latitudes = shape[1]
+
+    def along(block, shift):
+        return pltpu.roll(block, shift % latitudes, 1)
+
+    def one_level(z, carry):
+        column = lax.broadcasted_iota(jnp.int32, shape, 1)
+        last = column == latitudes - 1
+        first = column == 0
+        wet = (depth_ref[...] > z).astype(jnp.float32)
+        own = strip_ref[: shape[0]]
+        north_open = jnp.where(last, 0.0, wet * along(wet, -1))
+        north_flow = (v_ref[z] - BARO_GAIN * (along(own, -1) - own)) * north_open * (1.0 / 12.0)
+        north_mix = HORIZ_DIFF * north_open
+        for k in range(TRACERS):
+            masked = tracers_ref[k, z] * wet
+            north_one = jnp.where(last, 0.0, along(masked, -1))
+            pair = masked + north_one
+            south_pair = jnp.where(first, masked, along(pair, 1))
+            north_pair = jnp.where(last, 0.0, along(pair, -1))
+            face = 8.0 * pair - (south_pair + north_pair)
+            flux = north_flow * face - north_mix * (north_one - masked)
+            partial_ref[k, z] += wet * (along(flux, 1) - flux)
+        return carry
+
+    lax.fori_loop(0, tracers_ref.shape[1], one_level, 0)
+
+
 def solve_and_hand_over(
-    surface_old, surface_forcing, surface_coeff, ocean_mask, column_depth, tracers, low, high
+    surface_old,
+    surface_forcing,
+    surface_coeff,
+    ocean_mask,
+    column_depth,
+    tracers,
+    v_clinic,
+    low,
+    high,
 ):
     rows, columns = surface_old.shape
     count = lax.axis_size("lon")
@@ -248,7 +295,7 @@
     anywhere = pl.BlockSpec(memory_space=pl.ANY)
     return pl.pallas_call(
         solve_kernel,
-        in_specs=[vmem] * 6 + [anywhere] * 2,
+        in_specs=[vmem] * 5 + [anywhere] * 4,
         out_specs=[vmem] * 3 + [anywhere] * 2,
         out_shape=(
             jax.ShapeDtypeStruct((rows, columns), jnp.float32),
@@ -264,16 +311,27 @@
             pltpu.VMEM((count, RING, LANES), jnp.float32),
             pltpu.VMEM((count, RING, LANES), jnp.float32),
             pltpu.VMEM((SOLVER_ITERS, rows, columns), jnp.float32),
+            pltpu.VMEM(tracers.shape, jnp.float32),
+            pltpu.VMEM(v_clinic.shape, jnp.float32),
             pltpu.SemaphoreType.DMA((2, 2)),
             pltpu.SemaphoreType.DMA((2, 2)),
             pltpu.SemaphoreType.DMA((count,)),
             pltpu.SemaphoreType.DMA((count,)),
+            pltpu.SemaphoreType.DMA((2,)),
         ],
         compiler_params=pltpu.CompilerParams(
-            collective_id=0, has_side_effects=True, vmem_limit_bytes=20 * 2**20
+            collective_id=0, has_side_effects=True, vmem_limit_bytes=24 * 2**20
         ),
     )(
-        surface_old, surface_forcing, surface_coeff, ocean_mask, column_depth, tracers, low, high
+        surface_old,
+        surface_forcing,
+        surface_coeff,
+        ocean_mask,
+        column_depth,
+        tracers,
+        v_clinic,
+        low,
+        high,
     )
 
 
@@ -339,23 +397,17 @@
 
 
 def transport_kernel(
-    strip_ref, depth_ref, east_depth_ref, u_ref, v_ref, edge_ref, tracers_ref, partial_ref, out_ref
+    strip_ref, depth_ref, east_depth_ref, u_ref, edge_ref, tracers_ref, partial_ref, out_ref
 ):
     z = pl.program_id(0)
-    latitudes = depth_ref.shape[1]
     shape = depth_ref.shape
 
     def ring(block, shift):
         return pltpu.roll(block, shift % RING, 0)
 
-    def along(block, shift):
-        return pltpu.roll(block, shift % latitudes, 1)
-
-    column = lax.broadcasted_iota(jnp.int32, shape, 1)
     depth = depth_ref[...]
     wet = (depth > z).astype(jnp.float32)
     strip = strip_ref[...]
-    own = strip[: shape[0]]
     flow_edge = edge_ref[TRACERS, 0]
     east_depth = jnp.concatenate(
         [east_depth_ref[...].astype(jnp.float32), ring_edge(flow_edge)], axis=0
@@ -364,12 +416,6 @@
     u_ext = jnp.concatenate([u_ref[0], flow_edge], axis=0)
     east_flow = (u_ext - BARO_GAIN * (ring(strip, -1) - strip)) * east_open * (1.0 / 12.0)
     east_mix = HORIZ_DIFF * east_open
-    last = column == latitudes - 1
-    north_open = jnp.where(last, 0.0, wet * along(wet, -1))
-    north_flow = (v_ref[0] - BARO_GAIN * (along(own, -1) - own)) * north_open * (1.0 / 12.0)
-    north_mix = HORIZ_DIFF * north_open
-    first = column == 0
-
     for k in range(TRACERS):
         masked = tracers_ref[k, 0] * wet
         extended = jnp.concatenate([masked, edge_ref[k, 0]], axis=0)
@@ -378,13 +424,6 @@
         face = 8.0 * pair - (ring(pair, 1) + ring(pair, -1))
         flux = east_flow * face - east_mix * (east_one - extended)
         change = (ring(flux, 1) - flux)[: shape[0]]
-        north_one = jnp.where(last, 0.0, along(masked, -1))
-        pair = masked + north_one
-        south_pair = jnp.where(first, masked, along(pair, 1))
-        north_pair = jnp.where(last, 0.0, along(pair, -1))
-        face = 8.0 * pair - (south_pair + north_pair)
-        flux = north_flow * face - north_mix * (north_one - masked)
-        change = change + (along(flux, 1) - flux)
         out_ref[k, 0] = partial_ref[k, 0] + wet * change
 
 
@@ -392,7 +431,7 @@
     return pltpu.roll(flow_edge, 1, 0)
 
 
-def transport(strip, column_depth, east_depth, u_clinic, v_clinic, edges, tracers, partial):
+def transport(strip, column_depth, east_depth, u_clinic, edges, tracers, partial):
     count, levels, width, latitudes = tracers.shape
     whole = lambda shape: pl.BlockSpec(shape, lambda z: (0,) * len(shape))
     level = lambda rows: pl.BlockSpec((1, rows, latitudes), lambda z: (z, 0, 0))
@@ -405,7 +444,6 @@
             whole(column_depth.shape),
             whole(east_depth.shape),
             level(width),
-            level(width),
             pl.BlockSpec((count + 1, 1, RING - width, latitudes), lambda z: (0, z, 0, 0)),
             cut,
             cut,
@@ -413,7 +451,7 @@
         out_specs=cut,
         out_shape=jax.ShapeDtypeStruct(tracers.shape, jnp.float32),
         compiler_params=pltpu.CompilerParams(vmem_limit_bytes=40 * 2**20),
-    )(strip, column_depth, east_depth, u_clinic, v_clinic, edges, tracers, partial)
+    )(strip, column_depth, east_depth, u_clinic, edges, tracers, partial)
 
 
 def edge_blocks(column_depth, east_depth, u_clinic, tracers):
@@ -448,11 +486,19 @@
 ):
     low, high = edge_blocks(column_depth, east_depth, u_clinic, tracers)
     surface, strip, partial, low, high = solve_and_hand_over(
-        surface_old, surface_forcing, surface_coeff, ocean_mask, column_depth, tracers, low, high
+        surface_old,
+        surface_forcing,
+        surface_coeff,
+        ocean_mask,
+        column_depth,
+        tracers,
+        v_clinic,
+        low,
+        high,
     )
     edges = ring_of(low, high)
     tracers_new = transport(
-        strip, column_depth, east_depth, u_clinic, v_clinic, edges, tracers, partial
+        strip, column_depth, east_depth, u_clinic, edges, tracers, partial
     )
     return (surface, tracers_new)
 

time: 48.9 us -> 54.8 us (1.12)
  Pallas kernels: 38 us -> 44 us
    pallas_call x1, Pallas kernels: 23.7 us -> 35.2 us  [solve_and_hand_over(): pl.pallas_call(solve_kernel, in_specs=[vmem] * 5 + [anywhere] * 4, out_sp...]
    pallas_call x1, Pallas kernels: 14.3 us -> 8.78 us  [transport(): pl.pallas_call(transport_kernel, grid=(levels,), in_specs=[whole(strip.sh...]
where the time goes in v5:
time: 54.8 us; the launch traced here: 54.3 us
  Pallas kernels  44 us (80%)
  local copies, waits for them, and re-layouts  5.09 us (9%)
  other arithmetic  4.49 us (8%)
  between operations  0.81 us (1%)
    pallas_call x1, Pallas kernels, solve_and_hand_over(): pl.pallas_call(solve_kernel, in_specs=[vmem] * 5 + [anywhere] * 4, out_sp...  35.2 us
    pallas_call x1, Pallas kernels, transport(): pl.pallas_call(transport_kernel, grid=(levels,), in_specs=[whole(strip.sh...  8.78 us
    unnamed x21, local copies, waits for them, and re-layouts  3.35 us
    select_n x1, other arithmetic, masked(): return jnp.where(wet[None], tracers[:, :, where], 0.0)  2.79 us

profile of v5, /device:TPU:0, one launch (start us, length us, event | category | flops | bytes accessed | tf_op | source)
XLA Modules:
  0.0 54.3 jit_solution(1206462233142875623)
XLA Ops:
  0.6 0.0 copy-start.4
  0.6 0.0 copy-start.3
  0.7 0.0 copy-start.9
  0.7 0.0 copy-start.8
  0.7 0.0 copy-start.7
  0.7 0.0 copy-start.6
  0.7 0.8 %slice_convert_fusion = f32[1,512]{1,0:T(1,128)S(1)} fusion(s32[16,512]{1,0:T(8,128)} %east_depth_ref.1), kind=kLoop, calls=%fused_computation.8 | loop fusion | flops 512 | bytes 4096 | tf_op jit(solution)/shard_map/convert_element_type | solution.py:465
  1.5 0.7 %fusion = (s32[2,512]{1,0:T(2,128)S(1)}, s32[2,512]{1,0:T(2,128)S(1)}) fusion(s32[16,512]{1,0:T(8,128)} %depth_ref.3), kind=kLoop, calls=%fused_computation.9 | loop fusion | bytes 16384 | tf_op jit(solution)/shard_map/slice | solution.py:462
  2.2 1.0 %slice.21 = f32[16,1,512]{2,1,0:T(1,128)S(1)} slice(f32[16,16,512]{2,1,0:T(8,128)} %u_ref.1), slice={[0:16], [15:16], [0:512]} | slice | bytes 65536 | tf_op jit(solution)/shard_map/slice | solution.py:466
  3.2 0.1 maximum_bitcast_fusion
  3.3 0.1 iota_compare_fusion.1
  3.4 2.8 %slice_select_fusion = (f32[8,16,2,512]{3,2,1,0:T(2,128)S(1)}, f32[8,16,2,512]{3,2,1,0:T(2,128)S(1)}) fusion(f32[8,16,16,512]{3,2,1,0:T(8,128)} %tracers_ref.1, pred[16,2,512]{2,1,0:T(4,128)(4,1)S(1)} %get-tuple-element.16, pred[16,2,512]{2,1,0:T(4,128)(4,1)S(1)} %get-tuple-element.17), kind=kLoop, calls=%fused_computation.3 | loop fusion | flops 262144 | bytes 2129920 | tf_op jit(solution)/shard_map/jit(_where)/select_n | solution.py:463
  6.2 0.3 pad_maximum_fusion.low_ref
  6.5 0.0 copy-done.4
  6.5 0.0 copy-done.3
  6.5 0.0 copy-done.9
  6.5 0.0 copy-done.8
  6.5 0.0 copy-done.7
  6.5 0.0 copy-done.6
  6.5 0.0 copy-start
  6.5 2.2 %copy-done = f32[8,16,16,512]{3,2,1,0:T(8,128)S(1)} copy-done((f32[8,16,16,512]{3,2,1,0:T(8,128)S(1)}, f32[8,16,16,512]{3,2,1,0:T(8,128)}, u32[]{:S(2)}) %copy-start) | copy-done | bytes 4194328
  8.7 0.0 copy-start.1
  8.7 35.2 %shard_map.104 = (f32[32,256]{1,0:T(8,128)S(1)}, f32[24,512]{1,0:T(8,128)S(1)}, f32[8,16,16,512]{3,2,1,0:T(8,128)S(1)}, f32[9,16,2,512]{3,2,1,0:T(2,128)S(1)}, f32[8,16,2,512]{3,2,1,0:T(2,128)S(1)}) custom-call(f32[32,256]{1,0:T(8,128)S(1)} %copy-done.6, f32[32,256]{1,0:T(8,128)S(1)} %copy-done.7, f32[32,256]{1,0:T(8,128)S(1)} %copy-done.8, ...), custom_call_target="tpu_custom_call" | custom-call | tf_op jit(solution)/shard_map/pallas_call | solution.py:296
  43.9 0.0 copy-start.2
  43.9 0.0 copy-start.5
  43.9 0.5 select_maximum_fusion.edge_ref
  44.4 0.0 copy-done.1
  44.4 0.5 copy-done.2
  45.0 0.0 copy-done.5
  45.0 8.8 %shard_map.105 = f32[8,16,16,512]{3,2,1,0:T(8,128)} custom-call(f32[24,512]{1,0:T(8,128)S(1)} %get-tuple-element.8.strip_ref, s32[16,512]{1,0:T(8,128)S(1)} %copy-done.4, s32[16,512]{1,0:T(8,128)S(1)} %copy-done.5, f32[16,16,512]{2,1,0:T(8,128)S(1)} %copy-done.2, f32[9,16,8,512]{3,2,1,0:T(8,128)S(1)} %select_maximum_fusion.edge_ref, ...), custom_call_target="tpu_custom_call" | custom-call | tf_op jit(solution)/shard_map/pallas_call | solution.py:439
  53.7 0.6 %copy.12 = f32[32,256]{1,0:T(8,128)} copy(f32[32,256]{1,0:T(8,128)S(1)} %get-tuple-element.20) | data formatting | bytes 65536
  (1 shorter events, 0.0 us)
Async XLA Ops:
  0.6 5.8 %copy-start.4 = (s32[16,512]{1,0:T(8,128)S(1)}, s32[16,512]{1,0:T(8,128)}, u32[]{:S(2)}) copy-start(s32[16,512]{1,0:T(8,128)} %depth_ref.3) | copy-start | bytes 98308
  0.6 5.8 %copy-start.3 = (f32[16,16,512]{2,1,0:T(8,128)S(1)}, f32[16,16,512]{2,1,0:T(8,128)}, u32[]{:S(2)}) copy-start(f32[16,16,512]{2,1,0:T(8,128)} %v_hbm.1) | copy-start | bytes 1572868
  0.7 5.8 %copy-start.9 = (s32[32,256]{1,0:T(8,128)S(1)}, s32[32,256]{1,0:T(8,128)}, u32[]{:S(2)}) copy-start(s32[32,256]{1,0:T(8,128)} %mask_ref.1) | copy-start | bytes 98308
  0.7 5.8 %copy-start.8 = (f32[32,256]{1,0:T(8,128)S(1)}, f32[32,256]{1,0:T(8,128)}, u32[]{:S(2)}) copy-start(f32[32,256]{1,0:T(8,128)} %coeff_ref.1) | copy-start | bytes 98308
  0.7 5.8 %copy-start.7 = (f32[32,256]{1,0:T(8,128)S(1)}, f32[32,256]{1,0:T(8,128)}, u32[]{:S(2)}) copy-start(f32[32,256]{1,0:T(8,128)} %forcing_ref.1) | copy-start | bytes 98308
  0.7 5.8 %copy-start.6 = (f32[32,256]{1,0:T(8,128)S(1)}, f32[32,256]{1,0:T(8,128)}, u32[]{:S(2)}) copy-start(f32[32,256]{1,0:T(8,128)} %old_ref.1) | copy-start | bytes 98308
  6.5 2.2 %copy-start = (f32[8,16,16,512]{3,2,1,0:T(8,128)S(1)}, f32[8,16,16,512]{3,2,1,0:T(8,128)}, u32[]{:S(2)}) copy-start(f32[8,16,16,512]{3,2,1,0:T(8,128)} %tracers_ref.1) | copy-start | bytes 12582916
  8.7 35.7 %copy-start.1 = (f32[8,16,16,512]{3,2,1,0:T(8,128)S(1)}, f32[8,16,16,512]{3,2,1,0:T(8,128)}, u32[]{:S(2)}) copy-start(f32[8,16,16,512]{3,2,1,0:T(8,128)} %tracers_ref.1) | copy-start | bytes 12582916
  43.9 1.0 %copy-start.2 = (f32[16,16,512]{2,1,0:T(8,128)S(1)}, f32[16,16,512]{2,1,0:T(8,128)}, u32[]{:S(2)}) copy-start(f32[16,16,512]{2,1,0:T(8,128)} %u_ref.1) | copy-start | bytes 1572868
  43.9 1.0 %copy-start.5 = (s32[16,512]{1,0:T(8,128)S(1)}, s32[16,512]{1,0:T(8,128)}, u32[]{:S(2)}) copy-start(s32[16,512]{1,0:T(8,128)} %east_depth_ref.1) | copy-start | bytes 98308

commit v6 on v4

--- a/solution.py
+++ b/solution.py
@@ -113,10 +113,10 @@
 
 
 def solve_kernel(
-    old_ref, forcing_ref, coeff_ref, mask_ref, depth_ref, tracers_ref, low_ref, high_ref,
+    old_ref, forcing_ref, coeff_ref, mask_ref, depth_ref, tracers_hbm, low_ref, high_ref,
     surface_ref, strip_ref, partial_ref, low_out, high_out,
-    fields, below_in, above_in, send, recv, basis_kept,
-    edge_sems, band_sems, send_sems, recv_sems,
+    fields, below_in, above_in, send, recv, basis_kept, tracers_ref,
+    edge_sems, band_sems, send_sems, recv_sems, local_sem,
 ):
     count = lax.axis_size("lon")
     me = lax.axis_index("lon")
@@ -132,6 +132,8 @@
         return carry
 
     lax.fori_loop(1, count, greet, 0)
+    fetch = pltpu.make_async_copy(tracers_hbm, tracers_ref, local_sem)
+    fetch.start()
     fields[0] = coeff_ref[...] * old_ref[...] + forcing_ref[...]
     fields[1] = coeff_ref[...]
     fields[2] = mask_ref[...].astype(jnp.float32)
@@ -210,6 +212,7 @@
 
     lax.fori_loop(1, count, start_block, 0)
     recv[me] = send[me]
+    fetch.wait()
     column_terms(depth_ref, tracers_ref, partial_ref)
     lax.fori_loop(1, count, wait_block, 0)
     combine(recv, basis_kept, surface_ref, strip_ref)
@@ -248,7 +251,7 @@
     anywhere = pl.BlockSpec(memory_space=pl.ANY)
     return pl.pallas_call(
         solve_kernel,
-        in_specs=[vmem] * 6 + [anywhere] * 2,
+        in_specs=[vmem] * 5 + [pl.BlockSpec(memory_space=pltpu.HBM)] + [anywhere] * 2,
         out_specs=[vmem] * 3 + [anywhere] * 2,
         out_shape=(
             jax.ShapeDtypeStruct((rows, columns), jnp.float32),
@@ -264,13 +267,15 @@
             pltpu.VMEM((count, RING, LANES), jnp.float32),
             pltpu.VMEM((count, RING, LANES), jnp.float32),
             pltpu.VMEM((SOLVER_ITERS, rows, columns), jnp.float32),
+            pltpu.VMEM(tracers.shape, jnp.float32),
             pltpu.SemaphoreType.DMA((2, 2)),
             pltpu.SemaphoreType.DMA((2, 2)),
             pltpu.SemaphoreType.DMA((count,)),
             pltpu.SemaphoreType.DMA((count,)),
+            pltpu.SemaphoreType.DMA,
         ],
         compiler_params=pltpu.CompilerParams(
-            collective_id=0, has_side_effects=True, vmem_limit_bytes=20 * 2**20
+            collective_id=0, has_side_effects=True, vmem_limit_bytes=24 * 2**20
         ),
     )(
         surface_old, surface_forcing, surface_coeff, ocean_mask, column_depth, tracers, low, high

time: 48.9 us -> 48.9 us (level)
  no operation moved by 1% of the time
where the time goes in v6:
time: 48.9 us; the launch traced here: 48.5 us
  Pallas kernels  38 us (78%)
  local copies, waits for them, and re-layouts  5.24 us (11%)
  other arithmetic  4.48 us (9%)
  between operations  0.81 us (2%)
    pallas_call x1, Pallas kernels, solve_and_hand_over(): pl.pallas_call(solve_kernel, in_specs=[vmem] * 5 + [pl.BlockSpec(memory_s...  23.7 us
    pallas_call x1, Pallas kernels, transport(): pl.pallas_call(transport_kernel, grid=(levels,), in_specs=[whole(strip.sh...  14.3 us
    unnamed x21, local copies, waits for them, and re-layouts  3.5 us
    select_n x1, other arithmetic, masked(): return jnp.where(wet[None], tracers[:, :, where], 0.0)  2.8 us
    slice x1, local copies, waits for them, and re-layouts, edge_blocks(): flow = jnp.concatenate([ends, u_clinic[:, -1:]], axis=1)  0.98 us

profile of v6, /device:TPU:0, one launch (start us, length us, event | category | flops | bytes accessed | tf_op | source)
XLA Modules:
  0.0 48.5 jit_solution(13751922755911663409)
XLA Ops:
  0.6 0.0 copy-start.4
  0.6 0.0 copy-start.9
  0.7 0.0 copy-start.8
  0.7 0.0 copy-start.7
  0.7 0.0 copy-start.6
  0.7 0.8 %slice_convert_fusion = f32[1,512]{1,0:T(1,128)S(1)} fusion(s32[16,512]{1,0:T(8,128)} %east_depth_ref.1), kind=kLoop, calls=%fused_computation.8 | loop fusion | flops 512 | bytes 4096 | tf_op jit(solution)/shard_map/convert_element_type | solution.py:432
  1.4 0.7 %fusion = (s32[2,512]{1,0:T(2,128)S(1)}, s32[2,512]{1,0:T(2,128)S(1)}) fusion(s32[16,512]{1,0:T(8,128)} %depth_ref.3), kind=kLoop, calls=%fused_computation.9 | loop fusion | bytes 16384 | tf_op jit(solution)/shard_map/slice | solution.py:429
  2.2 1.0 %slice.21 = f32[16,1,512]{2,1,0:T(1,128)S(1)} slice(f32[16,16,512]{2,1,0:T(8,128)} %u_ref.1), slice={[0:16], [15:16], [0:512]} | slice | bytes 65536 | tf_op jit(solution)/shard_map/slice | solution.py:433
  3.2 0.1 maximum_bitcast_fusion
  3.3 0.1 iota_compare_fusion.1
  3.3 2.8 %slice_select_fusion = (f32[8,16,2,512]{3,2,1,0:T(2,128)S(1)}, f32[8,16,2,512]{3,2,1,0:T(2,128)S(1)}) fusion(f32[8,16,16,512]{3,2,1,0:T(8,128)} %tracers_ref.1, pred[16,2,512]{2,1,0:T(4,128)(4,1)S(1)} %get-tuple-element.16, pred[16,2,512]{2,1,0:T(4,128)(4,1)S(1)} %get-tuple-element.17), kind=kLoop, calls=%fused_computation.3 | loop fusion | flops 262144 | bytes 2129920 | tf_op jit(solution)/shard_map/jit(_where)/select_n | solution.py:430
  6.1 0.3 pad_maximum_fusion.low_ref
  6.4 0.0 copy-done.4
  6.5 0.0 copy-done.9
  6.5 0.0 copy-done.8
  6.5 0.0 copy-done.7
  6.5 0.0 copy-done.6
  6.5 0.0 copy-start
  6.5 2.2 %copy-done = f32[8,16,16,512]{3,2,1,0:T(8,128)S(1)} copy-done((f32[8,16,16,512]{3,2,1,0:T(8,128)S(1)}, f32[8,16,16,512]{3,2,1,0:T(8,128)}, u32[]{:S(2)}) %copy-start) | copy-done | bytes 4194328
  8.7 0.0 copy-start.1
  8.7 23.7 %shard_map.104 = (f32[32,256]{1,0:T(8,128)S(1)}, f32[24,512]{1,0:T(8,128)S(1)}, f32[8,16,16,512]{3,2,1,0:T(8,128)S(1)}, f32[9,16,2,512]{3,2,1,0:T(2,128)S(1)}, f32[8,16,2,512]{3,2,1,0:T(2,128)S(1)}) custom-call(f32[32,256]{1,0:T(8,128)S(1)} %copy-done.6, f32[32,256]{1,0:T(8,128)S(1)} %copy-done.7, f32[32,256]{1,0:T(8,128)S(1)} %copy-done.8, ...), custom_call_target="tpu_custom_call" | custom-call | tf_op jit(solution)/shard_map/pallas_call | solution.py:252
  32.4 0.0 copy-start.2
  32.4 0.0 copy-start.3
  32.4 0.0 copy-start.5
  32.4 0.5 %select_maximum_fusion.edge_ref = f32[9,16,8,512]{3,2,1,0:T(8,128)S(1)} fusion(f32[8,16,2,512]{3,2,1,0:T(2,128)S(1)} %get-tuple-element.9, f32[9,16,2,512]{3,2,1,0:T(2,128)S(1)} %get-tuple-element.10), kind=kLoop, calls=%fused_computation | loop fusion | flops 1769472 | bytes 3473408 | tf_op jit(solution)/shard_map/concatenate | solution.py:440
  32.9 0.0 copy-done.1
  32.9 0.5 %copy-done.2 = f32[16,16,512]{2,1,0:T(8,128)S(1)} copy-done((f32[16,16,512]{2,1,0:T(8,128)S(1)}, f32[16,16,512]{2,1,0:T(8,128)}, u32[]{:S(2)}) %copy-start.2) | copy-done | bytes 524312
  33.4 0.2 copy-done.3
  33.6 0.0 copy-done.5
  33.6 14.3 %shard_map.105 = f32[8,16,16,512]{3,2,1,0:T(8,128)} custom-call(f32[24,512]{1,0:T(8,128)S(1)} %get-tuple-element.8.strip_ref, s32[16,512]{1,0:T(8,128)S(1)} %copy-done.4, s32[16,512]{1,0:T(8,128)S(1)} %copy-done.5, f32[16,16,512]{2,1,0:T(8,128)S(1)} %copy-done.2, f32[16,16,512]{2,1,0:T(8,128)S(1)} %copy-done.3, ...), custom_call_target="tpu_custom_call" | custom-call | tf_op jit(solution)/shard_map/pallas_call | solution.py:405
  47.9 0.6 %copy.12 = f32[32,256]{1,0:T(8,128)} copy(f32[32,256]{1,0:T(8,128)S(1)} %get-tuple-element.20) | data formatting | bytes 65536
  (1 shorter events, 0.0 us)
Async XLA Ops:
  0.6 5.8 %copy-start.4 = (s32[16,512]{1,0:T(8,128)S(1)}, s32[16,512]{1,0:T(8,128)}, u32[]{:S(2)}) copy-start(s32[16,512]{1,0:T(8,128)} %depth_ref.3) | copy-start | bytes 98308
  0.6 5.8 %copy-start.9 = (s32[32,256]{1,0:T(8,128)S(1)}, s32[32,256]{1,0:T(8,128)}, u32[]{:S(2)}) copy-start(s32[32,256]{1,0:T(8,128)} %mask_ref.1) | copy-start | bytes 98308
  0.7 5.8 %copy-start.8 = (f32[32,256]{1,0:T(8,128)S(1)}, f32[32,256]{1,0:T(8,128)}, u32[]{:S(2)}) copy-start(f32[32,256]{1,0:T(8,128)} %coeff_ref.1) | copy-start | bytes 98308
  0.7 5.8 %copy-start.7 = (f32[32,256]{1,0:T(8,128)S(1)}, f32[32,256]{1,0:T(8,128)}, u32[]{:S(2)}) copy-start(f32[32,256]{1,0:T(8,128)} %forcing_ref.1) | copy-start | bytes 98308
  0.7 5.8 %copy-start.6 = (f32[32,256]{1,0:T(8,128)S(1)}, f32[32,256]{1,0:T(8,128)}, u32[]{:S(2)}) copy-start(f32[32,256]{1,0:T(8,128)} %old_ref.1) | copy-start | bytes 98308
  6.5 2.2 %copy-start = (f32[8,16,16,512]{3,2,1,0:T(8,128)S(1)}, f32[8,16,16,512]{3,2,1,0:T(8,128)}, u32[]{:S(2)}) copy-start(f32[8,16,16,512]{3,2,1,0:T(8,128)} %tracers_ref.1) | copy-start | bytes 12582916
  8.7 24.2 %copy-start.1 = (f32[8,16,16,512]{3,2,1,0:T(8,128)S(1)}, f32[8,16,16,512]{3,2,1,0:T(8,128)}, u32[]{:S(2)}) copy-start(f32[8,16,16,512]{3,2,1,0:T(8,128)} %tracers_ref.1) | copy-start | bytes 12582916
  32.4 1.0 %copy-start.2 = (f32[16,16,512]{2,1,0:T(8,128)S(1)}, f32[16,16,512]{2,1,0:T(8,128)}, u32[]{:S(2)}) copy-start(f32[16,16,512]{2,1,0:T(8,128)} %u_ref.1) | copy-start | bytes 1572868
  32.4 1.2 %copy-start.3 = (f32[16,16,512]{2,1,0:T(8,128)S(1)}, f32[16,16,512]{2,1,0:T(8,128)}, u32[]{:S(2)}) copy-start(f32[16,16,512]{2,1,0:T(8,128)} %v_ref.1) | copy-start | bytes 1572868
  32.4 1.2 %copy-start.5 = (s32[16,512]{1,0:T(8,128)S(1)}, s32[16,512]{1,0:T(8,128)}, u32[]{:S(2)}) copy-start(s32[16,512]{1,0:T(8,128)} %east_depth_ref.1) | copy-start | bytes 98308
